TPU v7x, 512 devices: a whole 4x8x8 slice. The times are simulated.
512 devices in a mesh: ctx: 64 (over y, x, core), kvh: 8 (over z).
Axes of the slice: x: 4, y: 8, z: 8, core: 2. Of those that a mesh axis runs over, the one named last changes fastest.
Arguments:
- queries: bfloat16 [24576, 4096], P('ctx', 'kvh'), may hold values from -200 to 200
- key_head_rows: bfloat16 [24576, 1024], P('ctx', 'kvh'), may hold values from -6 to 6
- value_head_rows: bfloat16 [24576, 1024], P('ctx', 'kvh'), may hold values from -6 to 6
- output_cotangent: bfloat16 [24576, 4096], P('ctx', 'kvh'), may hold values from -6 to 6
- projection_input: bfloat16 [24576, 8192], P('ctx', 'kvh'), may hold values from -6 to 6
- adapter_hidden_state: bfloat16 [24576, 64], P('ctx'), may hold values from -6 to 6
- adapter_up_weight: bfloat16 [64, 4096], P(None, 'kvh'), may hold values from -0.09375 to 0.09375
- document_block_lengths: int32 [32], replicated, may hold values from 1 to 12, 192 in all
Outputs:
- query_gradient: bfloat16 [24576, 4096], P('ctx', 'kvh')
- key_gradient: bfloat16 [24576, 1024], P('ctx', 'kvh')
- value_gradient: bfloat16 [24576, 1024], P('ctx', 'kvh')
- down_adapter_gradient: float32 [8192, 64], P('kvh')
- up_adapter_gradient: float32 [64, 4096], P(None, 'kvh')
Inputs may be any that keep to these rules, and one draw needn't show every extreme that they name: `document_block_lengths`: they sum to 192, and the longest document is exactly 12 blocks.
All inputs are finite; a program needn't handle non-finite values.
Results may differ from a plain program's by a relative error of at most 0.015.
Values may be sent and summed in bfloat16 or wider, within the bound.
A program may use at most 128 MiB of HBM per device.

v0:
```python
import jax
import jax.numpy as jnp
from jax import lax
from jax.sharding import PartitionSpec as P

HEAD_DIMENSION = 128
REACH = 4
BLOCK = 128


very_negative = -1e30


def from_behind(shard, axis, by):
    peers = lax.axis_size(axis)
    pairs = [(i, i + by) for i in range(peers) if 0 <= i + by < peers]
    return lax.ppermute(shard, axis, pairs)


def visit(distance, work_fn, carried):
    if distance == 0:
        return work_fn(carried)
    return work_fn(carried)


def shards(
    queries,
    key_head_rows,
    value_head_rows,
    output_cotangent,
    projection_input,
    adapter_hidden_state,
    adapter_up_weight,
    document_block_lengths,
):
    tokens = queries.shape[0]
    groups = key_head_rows.shape[1] // HEAD_DIMENSION
    head_count = queries.shape[1] // (groups * HEAD_DIMENSION)
    factor = HEAD_DIMENSION ** (-0.5)
    query_h = queries.reshape(tokens, groups, head_count, HEAD_DIMENSION)
    grad_out = output_cotangent.reshape(tokens, groups, head_count, HEAD_DIMENSION)
    stacked = jnp.stack(
        [
            key_head_rows.reshape(tokens, groups, HEAD_DIMENSION),
            value_head_rows.reshape(tokens, groups, HEAD_DIMENSION),
        ]
    )
    own_index = lax.axis_index("ctx")
    offsets = BLOCK * (jnp.cumsum(document_block_lengths) - document_block_lengths)
    query_pos = own_index * tokens + jnp.arange(tokens, dtype=jnp.int32)
    first_pos = jnp.max(
        jnp.where(offsets[None, :] <= query_pos[:, None], offsets[None, :], 0), axis=1
    )
    lowest = jnp.min(first_pos)
    window = [stacked]
    for distance in range(1, REACH + 1):
        window.append(from_behind(stacked, "ctx", distance))
    allowed = []
    is_live = []
    for distance in range(REACH + 1):
        positions = (own_index - distance) * tokens + jnp.arange(tokens, dtype=jnp.int32)
        inside = (positions[None, :] <= query_pos[:, None]) & (
            positions[None, :] >= first_pos[:, None]
        )
        allowed.append(inside[:, None, None, :])
        is_live.append((own_index - distance) * tokens + tokens - 1 >= lowest)
    row_shape = (tokens, groups, head_count, 1)
    scores = []
    running = (jnp.full(row_shape, very_negative, jnp.float32), jnp.zeros(row_shape, jnp.float32))
    for distance in range(REACH + 1):

        def absorb(carried, distance=distance):
            running_max, running_sum = carried
            tile = (
                jnp.einsum(
                    "tghd,sgd->tghs",
                    query_h,
                    window[distance][0],
                    preferred_element_type=jnp.float32,
                )
                * factor
            )
            masked = jnp.where(allowed[distance], tile, very_negative)
            newest = jnp.maximum(running_max, jnp.max(masked, axis=3, keepdims=True))
            running_sum = running_sum * jnp.exp(running_max - newest) + jnp.sum(
                jnp.exp(masked - newest), axis=3, keepdims=True
            )
            return (tile, newest, running_sum)

        tile, running_max, running_sum = visit(distance, absorb, running)
        running = (running_max, running_sum)
        scores.append(tile)
    log_total = running[0] + jnp.log(running[1])
    probs = []
    dprobs = []
    row_delta = jnp.zeros(row_shape, jnp.float32)
    for distance in range(REACH + 1):

        def weigh(carried, distance=distance):
            prob_tile = jnp.where(allowed[distance], jnp.exp(scores[distance] - log_total), 0.0)
            dprob_tile = jnp.einsum(
                "tghd,sgd->tghs", grad_out, window[distance][1], preferred_element_type=jnp.float32
            )
            return (
                prob_tile,
                dprob_tile,
                carried + jnp.sum(prob_tile * dprob_tile, axis=3, keepdims=True),
            )

        prob_tile, dprob_tile, row_delta = visit(distance, weigh, row_delta)
        probs.append(prob_tile)
        dprobs.append(dprob_tile)
    grad_query = jnp.zeros((tokens, groups, head_count, HEAD_DIMENSION), jnp.float32)
    pieces = []
    for distance in range(REACH + 1):

        def settle(carried, distance=distance):
            prob_tile = probs[distance]
            dscore = (prob_tile * (dprobs[distance] - row_delta)).astype(jnp.bfloat16)
            prob_low = prob_tile.astype(jnp.bfloat16)
            carried = carried + jnp.einsum(
                "tghs,sgd->tghd", dscore, window[distance][0], preferred_element_type=jnp.float32
            )
            grad_key = (
                jnp.einsum("tghs,tghd->sgd", dscore, query_h, preferred_element_type=jnp.float32)
                * factor
            )
            grad_value = jnp.einsum(
                "tghs,tghd->sgd", prob_low, grad_out, preferred_element_type=jnp.float32
            )
            return (carried, jnp.stack([grad_key, grad_value]))

        grad_query, piece = visit(distance, settle, grad_query)
        pieces.append(piece)
    summed = pieces[0]
    for distance in range(1, REACH + 1):
        summed = summed + from_behind(
            pieces[distance].astype(jnp.bfloat16), "ctx", -distance
        ).astype(jnp.float32)
    query_gradient = (
        (grad_query * factor)
        .astype(jnp.bfloat16)
        .reshape(tokens, groups * head_count * HEAD_DIMENSION)
    )
    key_gradient = summed[0].astype(jnp.bfloat16).reshape(tokens, groups * HEAD_DIMENSION)
    value_gradient = summed[1].astype(jnp.bfloat16).reshape(tokens, groups * HEAD_DIMENSION)
    blended_output = jnp.einsum(
        "qh,zh->qz", query_gradient, adapter_up_weight, preferred_element_type=jnp.float32
    )
    blended_output = lax.psum(blended_output, "kvh")
    blended_output_lowp = blended_output.astype(jnp.bfloat16)
    part_down = jnp.einsum(
        "tf,tr->fr", projection_input, blended_output_lowp, preferred_element_type=jnp.float32
    )
    partial_up_gradient = jnp.einsum(
        "sz,sq->zq", adapter_hidden_state, query_gradient, preferred_element_type=jnp.float32
    )
    part_down, partial_up_gradient = lax.psum((part_down, partial_up_gradient), "ctx")
    scale_norm_divisor = (tokens * lax.axis_size("ctx")) ** (-0.5)
    return (
        query_gradient,
        key_gradient,
        value_gradient,
        part_down * scale_norm_divisor,
        partial_up_gradient * scale_norm_divisor,
    )


def solution(mesh):
    placed = (
        P("ctx", "kvh"),
        P("ctx", "kvh"),
        P("ctx", "kvh"),
        P("ctx", "kvh"),
        P("ctx", "kvh"),
        P("ctx", None),
        P(None, "kvh"),
        P(),
    )
    return jax.shard_map(
        shards,
        mesh=mesh,
        in_specs=placed,
        out_specs=(
            P("ctx", "kvh"),
            P("ctx", "kvh"),
            P("ctx", "kvh"),
            P("kvh", None),
            P(None, "kvh"),
        ),
        check_vma=False,
    )
```

profile of v0, /device:TPU:1, one launch (start us, length us, event | category | flops | bytes accessed | tf_op | source)
XLA Modules:
  0.0 313.8 jit_solution(14772309649485969046)
XLA Ops:
  8.3 5.5 %collective-permute-start.3 = (bf16[2,384,1,128]{3,1,2,0:T(8,128)(2,1)S(1)}, bf16[2,384,1,128]{3,1,2,0:T(8,128)(2,1)S(1)}, u32[]{:S(2)}, u32[]{:S(2)}) collective-permute-start(bf16[2,384,1,128]{3,1,2,0:T(8,128)(2,1)S(1)} %pad_maximum_fusion), channel_id=1, source_target_pairs={{0,32},{8,40},{16,48},{24,56},{32,64},{40,72},{48,80},{56,88},{64,... | collective-permute-start | bytes 589832 | tf_op jit(solution)/shard_map/ppermute | solution.py:17
  13.8 4.0 %collective-permute-start.2 = (bf16[2,384,1,128]{3,1,2,0:T(8,128)(2,1)S(1)}, bf16[2,384,1,128]{3,1,2,0:T(8,128)(2,1)S(1)}, u32[]{:S(2)}, u32[]{:S(2)}) collective-permute-start(bf16[2,384,1,128]{3,1,2,0:T(8,128)(2,1)S(1)} %pad_maximum_fusion), channel_id=1, source_target_pairs={{0,24},{8,32},{16,40},{24,48},{32,56},{40,64},{48,72},{56,80},{64,... | collective-permute-start | bytes 589832 | tf_op jit(solution)/shard_map/ppermute | solution.py:17
  17.8 3.1 collective-permute-start.1
  20.9 1.9 collective-permute-start
  25.4 1.7 fusion.25
  33.0 1.2 fusion.111
  34.3 1.2 fusion.108
  35.5 1.2 fusion.105
  36.7 1.2 fusion.102
  37.9 1.3 fusion.77
  40.7 4.6 %fusion.9 = (f32[384,4]{0,1:T(4,128)S(1)}, f32[384,4]{0,1:T(4,128)S(1)}, f32[384,4]{0,1:T(4,128)S(1)}, f32[384,4]{0,1:T(4,128)S(1)}, f32[384,4]{0,1:T(4,128)S(1)}, /*index=5*/f32[384,384,4]{1,0,2:T(8,128)}) fusion(f32[384,384,4]{1,0,2:T(8,128)S(1)} %get-tuple-element.51, f32[384,4]{0,1:T(4,128)S(1)} %log_add_fusion, ...), kind=kOutput, calls=%fused_computation.17 | convolution fusion | flops 165732864 | bytes 24858624 | tf_op jit(solution)/shard_map/tghd,sgd->tghs/dot_general | solution.py:101
  45.3 6.3 %fusion.46 = (bf16[384,4,384]{0,2,1:T(8,128)(2,1)}, bf16[384,4,384]{0,2,1:T(8,128)(2,1)}, bf16[384,4,384]{0,2,1:T(8,128)(2,1)}, bf16[384,4,384]{0,2,1:T(8,128)(2,1)}, bf16[384,4,384]{0,2,1:T(8,128)(2,1)S(1)}) fusion(f32[384,384,4]{1,0,2:T(8,128)} %get-tuple-element.54, f32[384,384,4]{1,0,2:T(8,128)S(1)} %get-tuple-element.51, f32[384,4]{0,1:T(4,128)S(1)} %add_add_fusion, ...), kind=kLoop, calls=%fused_computation.73 | loop fusion | flops 17694720 | bytes 30240768 | tf_op jit(solution)/shard_map/reshape.65
  52.1 2.4 fusion.117
  54.5 1.1 fusion.116
  56.1 1.1 fusion.114
  60.6 29.2 %psum.21 = bf16[384,64]{0,1:T(8,128)(2,1)S(1)} all-reduce(f32[384,64]{0,1:T(8,128)S(1)} %fusion.192), channel_id=1, replica_groups=mesh['ctx'=64,'kvh'=8] {'kvh'}, use_global_device_ids=true, to_apply=%region_17.18 | all-reduce | flops 24576 | bytes 147456 | tf_op jit(solution)/shard_map/psum | solution.py:150
  90.8 9.7 %collective-permute-start.4 = (bf16[2,384,1,128]{3,1,2,0:T(8,128)(2,1)S(1)}, bf16[2,384,1,128]{3,1,2,0:T(8,128)(2,1)}, u32[]{:S(2)}, u32[]{:S(2)}) collective-permute-start(bf16[2,384,1,128]{3,1,2,0:T(8,128)(2,1)S(1)} %pad_maximum_fusion.1), channel_id=1, source_target_pairs={{8,0},{16,8},{24,16},{32,24},{40,32},{48,40},{56,48},{64,56},{72,6... | collective-permute-start | bytes 589832 | tf_op jit(solution)/shard_map/ppermute | solution.py:17
  101.3 1.3 collective-permute-start.5
  102.7 1.3 collective-permute-start.6
  104.9 1.3 collective-permute-start.7
  107.7 193.9 %all-reduce.3.cloned.1.call-done = (f32[1024,64]{0,1:T(8,128)}, f32[64,512]{1,0:T(8,128)}) async-done(((f32[1024,64]{0,1:T(8,128)}, f32[64,512]{1,0:T(8,128)}), (f32[1024,64]{0,1:T(8,128)}, f32[64,512]{1,0:T(8,128)})) %all-reduce.3.cloned.1.call-update) | async-done | bytes 393232 | tf_op jit(solution)/shard_map/psum | solution.py:158
  301.6 1.7 broadcast_multiply_fusion
  303.3 1.6 broadcast_multiply_fusion.1
  304.9 1.4 fusion.151
  (110 shorter events, 20.1 us)
Async XLA Ops:
  7.2 99.1 %copy-start = (bf16[384,1024]{1,0:T(8,128)(2,1)S(1)}, bf16[384,1024]{1,0:T(8,128)(2,1)}, u32[]{:S(2)}) copy-start(bf16[384,1024]{1,0:T(8,128)(2,1)} %param.12) | copy-start | bytes 2359300
  7.2 19.9 %copy-start.23 = (bf16[384,128]{1,0:T(8,128)(2,1)S(1)}, bf16[384,128]{1,0:T(8,128)(2,1)}, u32[]{:S(2)}) copy-start(bf16[384,128]{1,0:T(8,128)(2,1)} %param.10) | copy-start | bytes 294916
  7.2 19.9 %copy-start.4 = (bf16[384,512]{1,0:T(8,128)(2,1)S(1)}, bf16[384,512]{1,0:T(8,128)(2,1)}, u32[]{:S(2)}) copy-start(bf16[384,512]{1,0:T(8,128)(2,1)} %param.11) | copy-start | bytes 1179652
  7.2 294.4 %all-reduce.3.cloned.1.call-start = ((), (), s32[]{:S(2)}) async-start(), calls=%async_computation | async-start | bytes 786432 | tf_op jit(solution)/shard_map/psum | solution.py:158
  8.3 19.3 %collective-permute-start.3 = (bf16[2,384,1,128]{3,1,2,0:T(8,128)(2,1)S(1)}, bf16[2,384,1,128]{3,1,2,0:T(8,128)(2,1)S(1)}, u32[]{:S(2)}, u32[]{:S(2)}) collective-permute-start(bf16[2,384,1,128]{3,1,2,0:T(8,128)(2,1)S(1)} %pad_maximum_fusion), channel_id=1, source_target_pairs={{0,32},{8,40},{16,48},{24,56},{32,64},{40,72},{48,80},{56,88},{64,... | collective-permute-start | bytes 589832 | tf_op jit(solution)/shard_map/ppermute | solution.py:17
  13.8 14.4 %collective-permute-start.2 = (bf16[2,384,1,128]{3,1,2,0:T(8,128)(2,1)S(1)}, bf16[2,384,1,128]{3,1,2,0:T(8,128)(2,1)S(1)}, u32[]{:S(2)}, u32[]{:S(2)}) collective-permute-start(bf16[2,384,1,128]{3,1,2,0:T(8,128)(2,1)S(1)} %pad_maximum_fusion), channel_id=1, source_target_pairs={{0,24},{8,32},{16,40},{24,48},{32,56},{40,64},{48,72},{56,80},{64,... | collective-permute-start | bytes 589832 | tf_op jit(solution)/shard_map/ppermute | solution.py:17
  17.8 11.0 %collective-permute-start.1 = (bf16[2,384,1,128]{3,1,2,0:T(8,128)(2,1)S(1)}, bf16[2,384,1,128]{3,1,2,0:T(8,128)(2,1)S(1)}, u32[]{:S(2)}, u32[]{:S(2)}) collective-permute-start(bf16[2,384,1,128]{3,1,2,0:T(8,128)(2,1)S(1)} %pad_maximum_fusion), channel_id=1, source_target_pairs={{0,16},{8,24},{16,32},{24,40},{32,48},{40,56},{48,64},{56,72},{64,... | collective-permute-start | bytes 589832 | tf_op jit(solution)/shard_map/ppermute | solution.py:17
  20.9 8.9 %collective-permute-start = (bf16[2,384,1,128]{3,1,2,0:T(8,128)(2,1)S(1)}, bf16[2,384,1,128]{3,1,2,0:T(8,128)(2,1)S(1)}, u32[]{:S(2)}, u32[]{:S(2)}) collective-permute-start(bf16[2,384,1,128]{3,1,2,0:T(8,128)(2,1)S(1)} %pad_maximum_fusion), channel_id=1, source_target_pairs={{0,8},{8,16},{16,24},{24,32},{32,40},{40,48},{48,56},{56,64},{64,7... | collective-permute-start | bytes 589832 | tf_op jit(solution)/shard_map/ppermute | solution.py:17
  25.3 15.3 %copy-start.10 = (pred[384,384]{0,1:T(8,128)(4,1)}, pred[384,384]{0,1:T(8,128)(4,1)S(1)}, u32[]{:S(2)}) copy-start(pred[384,384]{0,1:T(8,128)(4,1)S(1)} %get-tuple-element.42) | copy-start | bytes 442372
  25.4 15.3 %copy-start.11 = (pred[384,384]{0,1:T(8,128)(4,1)}, pred[384,384]{0,1:T(8,128)(4,1)S(1)}, u32[]{:S(2)}) copy-start(pred[384,384]{0,1:T(8,128)(4,1)S(1)} %get-tuple-element.43) | copy-start | bytes 442372
  27.6 11.6 %copy-start.13 = (bf16[2,384,1,128]{3,1,2,0:T(8,128)(2,1)}, bf16[2,384,1,128]{3,1,2,0:T(8,128)(2,1)S(1)}, u32[]{:S(2)}) copy-start(bf16[2,384,1,128]{3,1,2,0:T(8,128)(2,1)S(1)} %collective-permute-done.3) | copy-start | bytes 589828
  28.2 11.5 %copy-start.15 = (bf16[2,384,1,128]{3,1,2,0:T(8,128)(2,1)}, bf16[2,384,1,128]{3,1,2,0:T(8,128)(2,1)S(1)}, u32[]{:S(2)}) copy-start(bf16[2,384,1,128]{3,1,2,0:T(8,128)(2,1)S(1)} %collective-permute-done.2) | copy-start | bytes 589828
  45.3 6.3 %copy-start.12 = (bf16[384,128]{1,0:T(8,128)(2,1)S(1)}, bf16[384,128]{1,0:T(8,128)(2,1)}, u32[]{:S(2)}) copy-start(bf16[384,128]{1,0:T(8,128)(2,1)} %param.9) | copy-start | bytes 294916
  51.6 4.0 %copy-start.2 = (bf16[384,4,384]{0,2,1:T(8,128)(2,1)}, bf16[384,4,384]{0,2,1:T(8,128)(2,1)S(1)}, u32[]{:S(2)}) copy-start(bf16[384,4,384]{0,2,1:T(8,128)(2,1)S(1)} %get-tuple-element.37) | copy-start | bytes 3538948
  52.1 4.0 %copy-start.6 = (bf16[384,4,384]{0,2,1:T(8,128)(2,1)S(1)}, bf16[384,4,384]{0,2,1:T(8,128)(2,1)}, u32[]{:S(2)}) copy-start(bf16[384,4,384]{0,2,1:T(8,128)(2,1)} %get-tuple-element.36) | copy-start | bytes 3538948
  58.9 30.9 %copy-start.28 = (bf16[384,64]{0,1:T(8,128)(2,1)S(1)}, bf16[384,64]{0,1:T(8,128)(2,1)}, u32[]{:S(2)}) copy-start(bf16[384,64]{0,1:T(8,128)(2,1)} %param.13) | copy-start | bytes 147460
  58.9 31.8 %copy-start.26 = (bf16[1,384,1,128]{3,1,2,0:T(8,128)(2,1)S(1)}, bf16[1,384,1,128]{3,1,2,0:T(8,128)(2,1)}, u32[]{:S(2)}) copy-start(bf16[1,384,1,128]{3,1,2,0:T(8,128)(2,1)} %fusion.111) | copy-start | bytes 294916
  59.4 41.0 %copy-start.25 = (bf16[1,384,1,128]{3,1,2,0:T(8,128)(2,1)S(1)}, bf16[1,384,1,128]{3,1,2,0:T(8,128)(2,1)}, u32[]{:S(2)}) copy-start(bf16[1,384,1,128]{3,1,2,0:T(8,128)(2,1)} %fusion.108) | copy-start | bytes 294916
  59.4 43.2 %copy-start.24 = (bf16[1,384,1,128]{3,1,2,0:T(8,128)(2,1)S(1)}, bf16[1,384,1,128]{3,1,2,0:T(8,128)(2,1)}, u32[]{:S(2)}) copy-start(bf16[1,384,1,128]{3,1,2,0:T(8,128)(2,1)} %fusion.105) | copy-start | bytes 294916
  60.4 46.9 %copy-start.3 = (bf16[384,4,384]{0,2,1:T(8,128)(2,1)S(1)}, bf16[384,4,384]{0,2,1:T(8,128)(2,1)}, u32[]{:S(2)}) copy-start(bf16[384,4,384]{0,2,1:T(8,128)(2,1)} %copy-done.2) | copy-start | bytes 3538948
  90.8 214.1 %collective-permute-start.4 = (bf16[2,384,1,128]{3,1,2,0:T(8,128)(2,1)S(1)}, bf16[2,384,1,128]{3,1,2,0:T(8,128)(2,1)}, u32[]{:S(2)}, u32[]{:S(2)}) collective-permute-start(bf16[2,384,1,128]{3,1,2,0:T(8,128)(2,1)S(1)} %pad_maximum_fusion.1), channel_id=1, source_target_pairs={{8,0},{16,8},{24,16},{32,24},{40,32},{48,40},{56,48},{64,56},{72,6... | collective-permute-start | bytes 589832 | tf_op jit(solution)/shard_map/ppermute | solution.py:17
  101.3 203.5 %collective-permute-start.5 = (bf16[2,384,1,128]{3,1,2,0:T(8,128)(2,1)S(1)}, bf16[2,384,1,128]{3,1,2,0:T(8,128)(2,1)}, u32[]{:S(2)}, u32[]{:S(2)}) collective-permute-start(bf16[2,384,1,128]{3,1,2,0:T(8,128)(2,1)S(1)} %pad_maximum_fusion.2), channel_id=1, source_target_pairs={{16,0},{24,8},{32,16},{40,24},{48,32},{56,40},{64,48},{72,56},{80,... | collective-permute-start | bytes 589832 | tf_op jit(solution)/shard_map/ppermute | solution.py:17
  102.7 202.2 %collective-permute-start.6 = (bf16[2,384,1,128]{3,1,2,0:T(8,128)(2,1)S(1)}, bf16[2,384,1,128]{3,1,2,0:T(8,128)(2,1)}, u32[]{:S(2)}, u32[]{:S(2)}) collective-permute-start(bf16[2,384,1,128]{3,1,2,0:T(8,128)(2,1)S(1)} %pad_maximum_fusion.3), channel_id=1, source_target_pairs={{24,0},{32,8},{40,16},{48,24},{56,32},{64,40},{72,48},{80,56},{88,... | collective-permute-start | bytes 589832 | tf_op jit(solution)/shard_map/ppermute | solution.py:17
  104.9 199.9 %collective-permute-start.7 = (bf16[2,384,1,128]{3,1,2,0:T(8,128)(2,1)S(1)}, bf16[2,384,1,128]{3,1,2,0:T(8,128)(2,1)}, u32[]{:S(2)}, u32[]{:S(2)}) collective-permute-start(bf16[2,384,1,128]{3,1,2,0:T(8,128)(2,1)S(1)} %pad_maximum_fusion.4), channel_id=1, source_target_pairs={{32,0},{40,8},{48,16},{56,24},{64,32},{72,40},{80,48},{88,56},{96,... | collective-permute-start | bytes 589832 | tf_op jit(solution)/shard_map/ppermute | solution.py:17
  (14 other events, 24.2 us)
Sparse Core Ops, SparseCore 0:
  107.4 194.2 all-reduce.2
where the time goes:
time: 316 us; the launch traced here: 314 us
  waiting for transfers between devices  194 us (61%)
  blocking collectives  29.2 us (9%)
  starting transfers between devices  28.1 us (9%)
  matrix products  26.2 us (8%)
  other arithmetic  18.2 us (6%)
  between operations  14.6 us (5%)
    psum x1, waiting for transfers between devices, shards(): lax.psum((part_down, partial_up_gradient), 'ctx')  194 us
    psum x1, blocking collectives, shards(): blended_output = lax.psum(blended_output, 'kvh')  29.2 us
    ppermute x8, starting transfers between devices, from_behind(): return lax.ppermute(shard, axis, pairs)  28 us
    another operation x4, other arithmetic  7.86 us
    dot_general x5, matrix products, weigh(): jnp.einsum('tghd,sgd->tghs', grad_out, window[distance][1], preferred_ele...  6.46 us
  transfers between devices with their start and end apart: 9, of which 2 were waited for; matrix products, arithmetic and copies ran while one was open for 4% of the time, Pallas kernels for 0%

commit v1 on v0

v1 whole, which is shorter than its diff:
```python
import functools
import math

import jax
import jax.numpy as jnp
from jax import lax
from jax.experimental import pallas as pl
from jax.experimental.pallas import tpu as pltpu
from jax.sharding import PartitionSpec as P

MESH = pl.DeviceIdType.MESH
HEAD = 128
HEADS = 4
BLOCK = 128
REACH = 4
TOK = 384
PER = TOK // BLOCK
SPAN = 12
ROWS = HEADS * BLOCK
NX, NCORE = 4, 2
FAR = 1e30
BF = jnp.bfloat16
F32 = jnp.float32

NT = (((1,), (1,)), ((), ()))
NN = (((1,), (0,)), ((), ()))


def dot(a, b, dims=NN):
    return lax.dot_general(a, b, dims, preferred_element_type=F32)


def fold8(tile, op):
    parts = tile.reshape(tile.shape[0] // 8, 8, tile.shape[1])
    return op(parts, axis=0)


def kernel(
    n_ctx, n_kvh, q_hbm, k_hbm, v_hbm, g_hbm, x_hbm, a_hbm, w_hbm, len_hbm,
    qg_hbm, dk_hbm, dv_hbm, down_hbm, up_hbm,
    q_ref, g_ref, x_ref, a_ref, w_ref, len_ref, kwin, vwin, kwin_t, s_ref, dp_ref, p_ref, ds_ref,
    top_ref, qg_ref, back_k, back_v, got_k, got_v, dk_ref, dv_ref,
    mix_own, mix_send, mix_got,
    down_own, up_own, down_send, up_send, down_a, up_a, down_y, up_y, down_fin, up_fin, down_out, up_out,
    in_sem, out_sem, halo_s, halo_r, back_s, back_r, mix_s, mix_r, rs_s, rs_r, ys_s, ys_r, ag_s, ag_r,
):
    n_y = n_ctx // (NX * NCORE)
    c = lax.axis_index("ctx")
    z = lax.axis_index("kvh")
    core = lax.rem(c, NCORE)
    x = lax.rem(c // NCORE, NX)
    y = c // (NX * NCORE)

    def at(yy, xx, cc):
        return ((yy * NX + xx) * NCORE + cc, z)

    def along(d):
        return (lax.rem(c + d + n_ctx, n_ctx), z)

    z_peers = [(lax.rem(z + o, n_kvh)) for o in range(1, n_kvh)]
    y_peers = [lax.rem(y + o, n_y) for o in range(1, n_y)]
    a_peers = [
        (lax.rem(x + dx, NX), lax.rem(core + dc, NCORE))
        for dx in range(NX) for dc in range(NCORE) if (dx, dc) != (0, 0)
    ]

    own = pl.ds(REACH * TOK, TOK)
    local = [
        pltpu.make_async_copy(src, dst, in_sem.at[i])
        for i, (src, dst) in enumerate([
            (q_hbm, q_ref), (k_hbm, kwin.at[own]), (g_hbm, g_ref), (v_hbm, vwin.at[own]),
            (len_hbm, len_ref), (w_hbm, w_ref), (a_hbm, a_ref), (x_hbm, x_ref),
        ])
    ]
    for cp in local:
        cp.start()
    lq, lk, lg, lv, llen, lw, la, lx = local

    barrier = pltpu.get_barrier_semaphore()
    greet = [along(d) for d in range(1, REACH + 1)] + [along(-d) for d in range(1, REACH + 1)]
    greet += [(c, zz) for zz in z_peers]
    greet += [at(yy, x, core) for yy in y_peers]
    greet += [at(y, xx, cc) for xx, cc in a_peers]
    for who in greet:
        pl.semaphore_signal(barrier, inc=1, device_id=who, device_id_type=MESH)
    pl.semaphore_wait(barrier, len(greet))

    halo = {}
    for d in range(1, REACH + 1):
        first = BLOCK if d == REACH else 0
        for j, (src, win) in enumerate([(k_hbm, kwin), (v_hbm, vwin)]):
            cp = pltpu.make_async_remote_copy(
                src_ref=src.at[pl.ds(first, TOK - first)],
                dst_ref=win.at[pl.ds((REACH - d) * TOK + first, TOK - first)],
                send_sem=halo_s.at[d - 1, j], recv_sem=halo_r.at[d - 1, j],
                device_id=along(d), device_id_type=MESH,
            )
            cp.start()
            halo[d, j] = cp

    llen.wait()
    firsts = [jnp.int32(0)] * PER
    start = jnp.int32(0)
    for doc in range(len_hbm.shape[0]):
        for i in range(PER):
            firsts[i] = jnp.where(start <= c * PER + i, start, firsts[i])
        start = start + len_ref[doc]

    def away(i, slot):
        block = c * PER + i + slot - (SPAN - 1)
        return jnp.where(block >= firsts[i], 0.0, FAR).astype(F32)

    def rows_of(ref, i):
        return jnp.concatenate(
            [ref[i * BLOCK:(i + 1) * BLOCK, h * HEAD:(h + 1) * HEAD] for h in range(HEADS)], axis=0
        )

    for i in range(PER):
        top_ref[i] = jnp.full((8, ROWS), -2.0 * FAR, F32)

    causal = (
        lax.broadcasted_iota(jnp.int32, (BLOCK, ROWS), 0)
        <= lax.broadcasted_iota(jnp.int32, (BLOCK, ROWS), 1) % BLOCK
    )

    def window(d, i):
        low = (REACH - d) * PER
        return max(low, i + 1), min(low + PER, i + SPAN + 1)

    def scores(d):
        for i in range(PER):
            lo, hi = window(d, i)
            if lo >= hi:
                continue
            s = dot(kwin[lo * BLOCK:hi * BLOCK], rows_of(q_ref, i), NT)
            top = top_ref[i]
            for w in range(lo, hi):
                slot = w - i - 1
                tile = s[(w - lo) * BLOCK:(w - lo + 1) * BLOCK]
                if slot == SPAN - 1:
                    tile = jnp.where(causal, tile, -FAR)
                s_ref[i, slot * BLOCK:(slot + 1) * BLOCK] = tile
                top = jnp.maximum(top, fold8(tile, jnp.max) - away(i, slot))
            top_ref[i] = top
        low = (REACH - d) * TOK + (BLOCK if d == REACH else 0)
        high = (REACH - d + 1) * TOK
        kwin_t[:, low:high] = kwin[low:high].T

    def dprobs(d):
        for i in range(PER):
            lo, hi = window(d, i)
            if lo >= hi:
                continue
            dp_ref[i, (lo - i - 1) * BLOCK:(hi - i - 1) * BLOCK] = dot(
                vwin[lo * BLOCK:hi * BLOCK], rows_of(g_ref, i), NT
            )

    lq.wait()
    lk.wait()
    scores(0)
    lg.wait()
    lv.wait()
    dprobs(0)
    for d in range(1, REACH + 1):
        halo[d, 0].wait_recv()
        scores(d)
        halo[d, 1].wait_recv()
        dprobs(d)

    factor = HEAD ** -0.5
    rate = factor * math.log2(math.e)
    STEP = 64
    lw.wait()
    mix_copies = []
    for i in range(PER):
        top = jnp.max(top_ref[i], axis=0, keepdims=True)

        def weigh(t, carry, i=i, top=top):
            total, delta = carry
            span = pl.ds(pl.multiple_of(t * STEP, STEP), STEP)
            level = top + away(i, t * STEP // BLOCK)
            p = jnp.exp2((s_ref[i, span] - level) * rate)
            s_ref[i, span] = p
            return total + fold8(p, jnp.sum), delta + fold8(p * dp_ref[i, span], jnp.sum)

        zero = jnp.zeros((8, ROWS), F32)
        total, delta = lax.fori_loop(0, SPAN * BLOCK // STEP, weigh, (zero, zero))
        share = 1.0 / jnp.sum(total, axis=0, keepdims=True)
        delta = jnp.sum(delta, axis=0, keepdims=True) * share

        def settle(t, carry, i=i, share=share, delta=delta):
            span = pl.ds(pl.multiple_of(t * STEP, STEP), STEP)
            p = s_ref[i, span] * share
            p_ref[i, span] = p.astype(BF)
            ds_ref[i, span] = (p * (dp_ref[i, span] - delta)).astype(BF)
            return carry

        lax.fori_loop(0, SPAN * BLOCK // STEP, settle, 0)
        dq = dot(kwin_t[:, (i + 1) * BLOCK:(i + 1 + SPAN) * BLOCK], ds_ref[i]) * factor
        for h in range(HEADS):
            qg_ref[i * BLOCK:(i + 1) * BLOCK, h * HEAD:(h + 1) * HEAD] = (
                dq[:, h * HEAD:(h + 1) * HEAD].T.astype(BF)
            )
        mixed = dot(w_ref[...], qg_ref[i * BLOCK:(i + 1) * BLOCK], NT)
        mix_own[:, i * BLOCK:(i + 1) * BLOCK] = mixed
        mix_send[i] = mixed.astype(BF)
        for o, zz in enumerate(z_peers):
            cp = pltpu.make_async_remote_copy(
                src_ref=mix_send.at[i], dst_ref=mix_got.at[i, o],
                send_sem=mix_s.at[i, o], recv_sem=mix_r.at[i, o],
                device_id=(c, zz), device_id_type=MESH,
            )
            cp.start()
            mix_copies.append(cp)

    out_qg = pltpu.make_async_copy(qg_ref, qg_hbm, out_sem.at[0])
    out_qg.start()

    def chunk(ref, xx, cc):
        width = ref.shape[1] // NCORE
        return ref.at[pl.ds(pl.multiple_of(xx * 16, 16), 16), pl.ds(pl.multiple_of(cc * width, 128), width)]

    def scatter(which, send, got):
        copies = []
        for o, (xx, cc) in enumerate(a_peers):
            cp = pltpu.make_async_remote_copy(
                src_ref=chunk(send, xx, cc), dst_ref=got.at[o],
                send_sem=rs_s.at[which, o], recv_sem=rs_r.at[which, o],
                device_id=at(y, xx, cc), device_id_type=MESH,
            )
            cp.start()
            copies.append(cp)
        return copies

    def exchange(which, copies, own_part, got, slots):
        for cp in copies:
            cp.wait_recv()
        part = chunk(own_part, x, core)[...]
        for o in range(len(a_peers)):
            part = part + got[o].astype(F32)
        slots[y] = part.astype(BF)
        out = []
        for o, yy in enumerate(y_peers):
            cp = pltpu.make_async_remote_copy(
                src_ref=slots.at[y], dst_ref=slots.at[y],
                send_sem=ys_s.at[which, o], recv_sem=ys_r.at[which, o],
                device_id=at(yy, x, core), device_id_type=MESH,
            )
            cp.start()
            out.append(cp)
        return out

    def gather(which, copies, slots, fin):
        for cp in copies:
            cp.wait_recv()
        part = slots[0].astype(F32)
        for yy in range(1, n_y):
            part = part + slots[yy].astype(F32)
        mine = chunk(fin, x, core)
        mine[...] = part.astype(BF)
        out = []
        for o, (xx, cc) in enumerate(a_peers):
            cp = pltpu.make_async_remote_copy(
                src_ref=mine, dst_ref=mine,
                send_sem=ag_s.at[which, o], recv_sem=ag_r.at[which, o],
                device_id=at(y, xx, cc), device_id_type=MESH,
            )
            cp.start()
            out.append(cp)
        return out

    la.wait()
    up = dot(a_ref[...], qg_ref[...])
    up_own[...] = up
    up_send[...] = up.astype(BF)
    up_rs = scatter(0, up_send, up_a)

    def ranges(d):
        low = (REACH - d) * PER
        dk = jnp.zeros((TOK, HEAD), F32)
        dv = jnp.zeros((TOK, HEAD), F32)
        parts_k, parts_v = [None] * PER, [None] * PER
        for i in range(PER):
            lo, hi = window(d, i)
            if lo >= hi:
                continue
            span = slice((lo - i - 1) * BLOCK, (hi - i - 1) * BLOCK)
            k_part = dot(ds_ref[i, span], rows_of(q_ref, i))
            v_part = dot(p_ref[i, span], rows_of(g_ref, i))
            for w in range(lo, hi):
                at_w = slice((w - lo) * BLOCK, (w - lo + 1) * BLOCK)
                b = w - low
                parts_k[b] = k_part[at_w] if parts_k[b] is None else parts_k[b] + k_part[at_w]
                parts_v[b] = v_part[at_w] if parts_v[b] is None else parts_v[b] + v_part[at_w]
        return parts_k, parts_v

    back = []
    for d in range(REACH, 0, -1):
        parts = ranges(d)
        first = BLOCK if d == REACH else 0
        for j, (buf, got) in enumerate([(back_k, got_k), (back_v, got_v)]):
            for b in range(first // BLOCK, PER):
                value = parts[j][b] * factor if j == 0 else parts[j][b]
                buf[d - 1, b * BLOCK:(b + 1) * BLOCK] = value.astype(BF)
            cp = pltpu.make_async_remote_copy(
                src_ref=buf.at[d - 1, pl.ds(first, TOK - first)],
                dst_ref=got.at[d - 1, pl.ds(first, TOK - first)],
                send_sem=back_s.at[d - 1, j], recv_sem=back_r.at[d - 1, j],
                device_id=along(-d), device_id_type=MESH,
            )
            cp.start()
            back.append(cp)

    up_ys = exchange(0, up_rs, up_own, up_a, up_y)

    parts_k, parts_v = ranges(0)

    for cp in mix_copies:
        cp.wait_recv()
    lx.wait()
    mixed = mix_own[...]
    for o in range(n_kvh - 1):
        mixed = mixed + jnp.concatenate([mix_got[i, o].astype(F32) for i in range(PER)], axis=1)
    down = dot(mixed.astype(BF), x_ref[...])
    down_own[...] = down
    down_send[...] = down.astype(BF)
    down_rs = scatter(1, down_send, down_a)

    up_ag = gather(0, up_ys, up_y, up_fin)
    down_ys = exchange(1, down_rs, down_own, down_a, down_y)

    for cp in back:
        cp.wait_recv()
    for b in range(PER):
        rows = slice(b * BLOCK, (b + 1) * BLOCK)
        sum_k, sum_v = parts_k[b] * factor, parts_v[b]
        for d in range(1, REACH + 1):
            if d == REACH and b == 0:
                continue
            sum_k = sum_k + got_k[d - 1, rows].astype(F32)
            sum_v = sum_v + got_v[d - 1, rows].astype(F32)
        dk_ref[rows] = sum_k.astype(BF)
        dv_ref[rows] = sum_v.astype(BF)
    out_dk = pltpu.make_async_copy(dk_ref, dk_hbm, out_sem.at[1])
    out_dv = pltpu.make_async_copy(dv_ref, dv_hbm, out_sem.at[2])
    out_dk.start()
    out_dv.start()

    down_ag = gather(1, down_ys, down_y, down_fin)
    scale = (TOK * n_ctx) ** -0.5
    for cp in up_ag:
        cp.wait_recv()
    up_out[...] = up_fin[...].astype(F32) * scale
    out_up = pltpu.make_async_copy(up_out, up_hbm, out_sem.at[3])
    out_up.start()
    for cp in down_ag:
        cp.wait_recv()
    down_out[...] = down_fin[...].astype(F32) * scale
    out_down = pltpu.make_async_copy(down_out, down_hbm, out_sem.at[4])
    out_down.start()

    for group in (list(halo.values()), back, mix_copies, up_rs, down_rs, up_ys, down_ys, up_ag, down_ag):
        for cp in group:
            cp.wait_send()
    for cp in (out_qg, out_dk, out_dv, out_up, out_down):
        cp.wait()


def shards(n_ctx, n_kvh, q, k, v, g, proj, hidden, weight, lengths):
    n_y = n_ctx // (NX * NCORE)
    n_a = NX * NCORE - 1
    feats, rank = proj.shape[1], hidden.shape[1]
    wide = q.shape[1]
    vm = pltpu.VMEM
    dma = pltpu.SemaphoreType.DMA
    win = (REACH + 1) * TOK
    anywhere = pl.BlockSpec(memory_space=pl.ANY)
    zs, ys = max(n_kvh - 1, 1), max(n_y - 1, 1)
    outs = pl.pallas_call(
        functools.partial(kernel, n_ctx, n_kvh),
        out_shape=(
            jax.ShapeDtypeStruct(q.shape, BF),
            jax.ShapeDtypeStruct(k.shape, BF),
            jax.ShapeDtypeStruct(v.shape, BF),
            jax.ShapeDtypeStruct((rank, feats), F32),
            jax.ShapeDtypeStruct((rank, wide), F32),
        ),
        in_specs=[anywhere] * 8,
        out_specs=(anywhere,) * 5,
        scratch_shapes=[
            vm(q.shape, BF), vm(g.shape, BF), vm(proj.shape, BF), vm((rank, TOK), BF), vm(weight.shape, BF),
            pltpu.SMEM(lengths.shape, jnp.int32),
            vm((win, HEAD), BF), vm((win, HEAD), BF), vm((HEAD, win), BF),
            vm((PER, SPAN * BLOCK, ROWS), F32), vm((PER, SPAN * BLOCK, ROWS), F32),
            vm((PER, SPAN * BLOCK, ROWS), BF), vm((PER, SPAN * BLOCK, ROWS), BF),
            vm((PER, 8, ROWS), F32), vm(q.shape, BF),
            vm((REACH, TOK, HEAD), BF), vm((REACH, TOK, HEAD), BF),
            vm((REACH, TOK, HEAD), BF), vm((REACH, TOK, HEAD), BF),
            vm(k.shape, BF), vm(v.shape, BF),
            vm((rank, TOK), F32), vm((PER, rank, BLOCK), BF), vm((PER, zs, rank, BLOCK), BF),
            vm((rank, feats), F32), vm((rank, wide), F32), vm((rank, feats), BF), vm((rank, wide), BF),
            vm((n_a, 16, feats // NCORE), BF), vm((n_a, 16, wide // NCORE), BF),
            vm((n_y, 16, feats // NCORE), BF), vm((n_y, 16, wide // NCORE), BF),
            vm((rank, feats), BF), vm((rank, wide), BF),
            vm((rank, feats), F32), vm((rank, wide), F32),
            dma((8,)), dma((5,)), dma((REACH, 2)), dma((REACH, 2)), dma((REACH, 2)), dma((REACH, 2)),
            dma((PER, zs)), dma((PER, zs)), dma((2, n_a)), dma((2, n_a)), dma((2, ys)), dma((2, ys)),
            dma((2, n_a)), dma((2, n_a)),
        ],
        compiler_params=pltpu.CompilerParams(
            collective_id=0, has_side_effects=True, vmem_limit_bytes=56 * 2**20
        ),
        cost_estimate=pl.CostEstimate(flops=3_200_000_000, bytes_accessed=4_000_000, transcendentals=2_400_000),
        name="attention_backward",
    )(q, k, v, g, proj, hidden.T, weight, lengths)
    qg, dk, dv, down, up = outs
    return qg, dk, dv, down.T, up


def solution(mesh):
    n_ctx, n_kvh = mesh.shape["ctx"], mesh.shape["kvh"]
    both = P("ctx", "kvh")
    return jax.shard_map(
        functools.partial(shards, n_ctx, n_kvh),
        mesh=mesh,
        in_specs=(both, both, both, both, both, P("ctx", None), P(None, "kvh"), P()),
        out_specs=(both, both, both, P("kvh", None), P(None, "kvh")),
        check_vma=False,
    )
```

time: 316 us -> 78.6 us (0.25)
  waiting for transfers between devices: 194 us -> 0 us
  Pallas kernels: 0 us -> 73 us
  blocking collectives: 29.2 us -> 0 us
  starting transfers between devices: 28.1 us -> 0 us
  matrix products: 26.2 us -> 0 us
  other arithmetic: 18.2 us -> 0 us
  between operations: 14.6 us -> 0.66 us
    psum x1 -> x0, waiting for transfers between devices: 194 us -> none  [shards(): lax.psum((part_down, partial_up_gradient), 'ctx')]
    pallas_call x0 -> x1, Pallas kernels: none -> 73 us  [shards(): pl.pallas_call(functools.partial(kernel, n_ctx, n_kvh), out_shape=(jax.Sh...]
    psum x1 -> x0, blocking collectives: 29.2 us -> none  [shards(): blended_output = lax.psum(blended_output, 'kvh')]
    ppermute x8 -> x0, starting transfers between devices: 28 us -> none  [from_behind(): return lax.ppermute(shard, axis, pairs)]
    dot_general x28 -> x0, matrix products: 26.2 us -> none  [the longest x5 6.46 us: weigh(): jnp.einsum('tghd,sgd->tghs', grad_out, window[distance][1], preferred_ele...]
    another operation x9 -> x0, other arithmetic: 10.8 us -> none
    mul x3 -> x0, other arithmetic: 3.91 us -> none  [the longest x1 1.68 us: shards(): part_down * scale_norm_divisor]
  transfers between devices with their start and end apart: 9 -> 0, of which waited for: 2 -> 0; matrix products, arithmetic and copies ran while one was open for 4% -> 0% of each run, Pallas kernels for 0% -> 0%
where the time goes in v1:
time: 78.6 us; the launch traced here: 78.4 us
  Pallas kernels  73 us (93%)
  local copies, waits for them, and re-layouts  4.75 us (6%)
    pallas_call x1, Pallas kernels, shards(): pl.pallas_call(functools.partial(kernel, n_ctx, n_kvh), out_shape=(jax.Sh...  73 us
    unnamed x13, local copies, waits for them, and re-layouts  4.75 us

profile of v1, /device:TPU:1, one launch (start us, length us, event | category | flops | bytes accessed | tf_op | source)
XLA Modules:
  0.0 78.4 jit_solution(13293434542918534132)
XLA Ops:
  0.6 73.0 %attention_backward.1 = (bf16[384,512]{1,0:T(8,128)(2,1)}, bf16[384,128]{1,0:T(8,128)(2,1)}, bf16[384,128]{1,0:T(8,128)(2,1)}, f32[64,1024]{1,0:T(8,128)}, f32[64,512]{1,0:T(8,128)}) custom-call(bf16[384,512]{1,0:T(8,128)(2,1)} %q_hbm.1, bf16[384,128]{1,0:T(8,128)(2,1)} %k_hbm.1, bf16[384,128]{1,0:T(8,128)(2,1)} %v_hbm.1, bf16[384,512]{1,0:T(8,128)(2,1)} %g_hbm.1, ...), custom_call_target="tpu_custom_call" | custom-call | flops 3200000000 | bytes 4000000 | tf_op jit(solution)/shard_map/attention_backward/pallas_call | solution.py:379
  73.6 0.0 copy-start.3
  73.6 0.0 copy-start.2
  73.6 1.8 %copy.18 = bf16[384,512]{1,0:T(8,128)(2,1)} copy(bf16[384,512]{1,0:T(8,128)(2,1)} %get-tuple-element.20) | data formatting | bytes 786432
  75.4 0.0 copy-done.3
  75.5 0.0 copy-start
  75.5 0.6 copy.19
  76.1 0.0 copy-done.2
  76.1 0.6 copy.20
  76.7 0.0 copy-done
  76.7 0.0 copy-start.1
  76.7 0.7 copy.21
  77.4 0.3 copy-done.1
  77.7 0.7 copy.22
Async XLA Ops:
  73.6 1.8 %copy-start.3 = (bf16[384,128]{1,0:T(8,128)(2,1)S(1)}, bf16[384,128]{1,0:T(8,128)(2,1)}, u32[]{:S(2)}) copy-start(bf16[384,128]{1,0:T(8,128)(2,1)} %get-tuple-element.21) | copy-start | bytes 294916
  73.6 2.5 %copy-start.2 = (bf16[384,128]{1,0:T(8,128)(2,1)S(1)}, bf16[384,128]{1,0:T(8,128)(2,1)}, u32[]{:S(2)}) copy-start(bf16[384,128]{1,0:T(8,128)(2,1)} %get-tuple-element.22) | copy-start | bytes 294916
  75.5 1.3 %copy-start = (f32[64,1024]{1,0:T(8,128)S(1)}, f32[64,1024]{1,0:T(8,128)}, u32[]{:S(2)}) copy-start(f32[64,1024]{1,0:T(8,128)} %get-tuple-element.13) | copy-start | bytes 786436
  76.7 1.0 %copy-start.1 = (f32[64,512]{1,0:T(8,128)S(1)}, f32[64,512]{1,0:T(8,128)}, u32[]{:S(2)}) copy-start(f32[64,512]{1,0:T(8,128)} %get-tuple-element.24) | copy-start | bytes 393220

commit v2 on v1

--- a/solution.py
+++ b/solution.py
@@ -37,12 +37,12 @@
 
 def kernel(
     n_ctx, n_kvh, q_hbm, k_hbm, v_hbm, g_hbm, x_hbm, a_hbm, w_hbm, len_hbm,
-    qg_hbm, dk_hbm, dv_hbm, down_hbm, up_hbm,
+    qg_ref, dk_ref, dv_ref, down_out, up_out,
     q_ref, g_ref, x_ref, a_ref, w_ref, len_ref, kwin, vwin, kwin_t, s_ref, dp_ref, p_ref, ds_ref,
-    top_ref, qg_ref, back_k, back_v, got_k, got_v, dk_ref, dv_ref,
+    top_ref, near, back, got,
     mix_own, mix_send, mix_got,
-    down_own, up_own, down_send, up_send, down_a, up_a, down_y, up_y, down_fin, up_fin, down_out, up_out,
-    in_sem, out_sem, halo_s, halo_r, back_s, back_r, mix_s, mix_r, rs_s, rs_r, ys_s, ys_r, ag_s, ag_r,
+    down_own, up_own, down_send, up_send, down_a, up_a, down_y, up_y, down_fin, up_fin,
+    in_sem, halo_s, halo_r, back_s, back_r, mix_s, mix_r, rs_s, rs_r, ys_s, ys_r, ag_s, ag_r,
 ):
     n_y = n_ctx // (NX * NCORE)
     c = lax.axis_index("ctx")
@@ -77,7 +77,7 @@
     lq, lk, lg, lv, llen, lw, la, lx = local
 
     barrier = pltpu.get_barrier_semaphore()
-    greet = [along(d) for d in range(1, REACH + 1)] + [along(-d) for d in range(1, REACH + 1)]
+    greet = [along(d) for d in (1, 2, 3, -1, -2, -3)]
     greet += [(c, zz) for zz in z_peers]
     greet += [at(yy, x, core) for yy in y_peers]
     greet += [at(y, xx, cc) for xx, cc in a_peers]
@@ -85,18 +85,46 @@
         pl.semaphore_signal(barrier, inc=1, device_id=who, device_id_type=MESH)
     pl.semaphore_wait(barrier, len(greet))
 
-    halo = {}
-    for d in range(1, REACH + 1):
+    mate = along(1 - 2 * core)
+    first_core, second_core = core == 0, core == 1
+
+    def slot_rows(d, first=0):
+        return pl.ds((REACH - d) * TOK + first, TOK - first)
+
+    def forward(n, j, src, d, to, first=0):
+        return pltpu.make_async_remote_copy(
+            src_ref=src, dst_ref=(kwin, vwin)[j].at[slot_rows(d, first)],
+            send_sem=halo_s.at[n, j], recv_sem=halo_r.at[d - 1, j], device_id=to, device_id_type=MESH,
+        )
+
+    def held(j, d, first=0):
+        return (kwin, vwin)[j].at[slot_rows(d, first)]
+
+    def own_next(j):
+        return forward(0, j, (k_hbm, v_hbm)[j], 1, along(1))
+
+    def own_far(j):
+        return forward(1, j, (k_hbm, v_hbm)[j], 3, along(3))
+
+    def pass_mate(j, d):
+        return forward(2, j, held(j, d), 2, mate)
+
+    def pass_chip(j):
+        return forward(3, j, held(j, 1), 3, along(2))
+
+    def pass_last(j):
+        return forward(4, j, held(j, 3, BLOCK), REACH, along(1), BLOCK)
+
+    def arrived(j, d):
         first = BLOCK if d == REACH else 0
-        for j, (src, win) in enumerate([(k_hbm, kwin), (v_hbm, vwin)]):
-            cp = pltpu.make_async_remote_copy(
-                src_ref=src.at[pl.ds(first, TOK - first)],
-                dst_ref=win.at[pl.ds((REACH - d) * TOK + first, TOK - first)],
-                send_sem=halo_s.at[d - 1, j], recv_sem=halo_r.at[d - 1, j],
-                device_id=along(d), device_id_type=MESH,
-            )
-            cp.start()
-            halo[d, j] = cp
+        forward(0, j, held(j, d, first), d, along(1), first).wait_recv()
+
+    for j in range(2):
+        own_next(j).start()
+
+        @pl.when(first_core)
+        def _(j=j):
+            own_far(j).start()
 
     llen.wait()
     firsts = [jnp.int32(0)] * PER
@@ -161,11 +189,46 @@
     lg.wait()
     lv.wait()
     dprobs(0)
-    for d in range(1, REACH + 1):
-        halo[d, 0].wait_recv()
-        scores(d)
-        halo[d, 1].wait_recv()
-        dprobs(d)
+
+    @pl.when(second_core)
+    def _():
+        for j in range(2):
+            arrived(j, 1)
+        scores(1)
+        dprobs(1)
+        for j in range(2):
+            arrived(j, 3)
+            pass_last(j).start()
+            pass_mate(j, 3).start()
+        scores(3)
+        dprobs(3)
+
+    @pl.when(first_core)
+    def _():
+        for j in range(2):
+            arrived(j, 1)
+            pass_chip(j).start()
+            pass_mate(j, 1).start()
+        scores(1)
+        dprobs(1)
+
+    for j in range(2):
+        arrived(j, 2)
+    scores(2)
+    dprobs(2)
+
+    @pl.when(first_core)
+    def _():
+        for j in range(2):
+            arrived(j, 3)
+            pass_last(j).start()
+        scores(3)
+        dprobs(3)
+
+    arrived(0, REACH)
+    scores(REACH)
+    arrived(1, REACH)
+    dprobs(REACH)
 
     factor = HEAD ** -0.5
     rate = factor * math.log2(math.e)
@@ -212,9 +275,6 @@
             )
             cp.start()
             mix_copies.append(cp)
-
-    out_qg = pltpu.make_async_copy(qg_ref, qg_hbm, out_sem.at[0])
-    out_qg.start()
 
     def chunk(ref, xx, cc):
         width = ref.shape[1] // NCORE
@@ -294,26 +354,55 @@
                 parts_v[b] = v_part[at_w] if parts_v[b] is None else parts_v[b] + v_part[at_w]
         return parts_k, parts_v
 
-    back = []
-    for d in range(REACH, 0, -1):
+    def store(d):
         parts = ranges(d)
         first = BLOCK if d == REACH else 0
-        for j, (buf, got) in enumerate([(back_k, got_k), (back_v, got_v)]):
+        for j in range(2):
             for b in range(first // BLOCK, PER):
                 value = parts[j][b] * factor if j == 0 else parts[j][b]
-                buf[d - 1, b * BLOCK:(b + 1) * BLOCK] = value.astype(BF)
-            cp = pltpu.make_async_remote_copy(
-                src_ref=buf.at[d - 1, pl.ds(first, TOK - first)],
-                dst_ref=got.at[d - 1, pl.ds(first, TOK - first)],
-                send_sem=back_s.at[d - 1, j], recv_sem=back_r.at[d - 1, j],
-                device_id=along(-d), device_id_type=MESH,
-            )
-            cp.start()
-            back.append(cp)
+                near[d, j, b * BLOCK:(b + 1) * BLOCK] = value.astype(near.dtype)
+
+    def send_back(n, src, slot, to, first=0):
+        rows = pl.ds(first, TOK - first)
+        return pltpu.make_async_remote_copy(
+            src_ref=src.at[:, rows], dst_ref=got.at[slot, :, rows],
+            send_sem=back_s.at[n], recv_sem=back_r.at[slot], device_id=to, device_id_type=MESH,
+        )
+
+    def came_back(slot, first=0):
+        send_back(0, got.at[slot], slot, along(-1), first).wait_recv()
+
+    back_4 = send_back(0, back.at[0], 0, along(-1), BLOCK)
+    back_2 = send_back(1, back.at[1], 1, mate)
+    back_1 = send_back(2, back.at[2], 2, along(-1))
+    back_3 = send_back(2, back.at[2], 3, along(-2))
+    last_0 = send_back(3, back.at[3], 4, along(-1))
+    last_1 = send_back(3, back.at[3], 4, along(-3))
+
+    store(REACH)
+    back[0, :, BLOCK:] = near[REACH, :, BLOCK:].astype(BF)
+    back_4.start()
+    store(2)
+    back[1] = near[2].astype(BF)
+    back_2.start()
+    store(1)
+    store(3)
+
+    @pl.when(second_core)
+    def _():
+        back[2] = near[1].astype(BF)
+        back_1.start()
+
+    @pl.when(first_core)
+    def _():
+        came_back(0, BLOCK)
+        back[2, :, :BLOCK] = near[3, :, :BLOCK].astype(BF)
+        back[2, :, BLOCK:] = (near[3, :, BLOCK:] + got[0, :, BLOCK:].astype(F32)).astype(BF)
+        back_3.start()
 
     up_ys = exchange(0, up_rs, up_own, up_a, up_y)
 
-    parts_k, parts_v = ranges(0)
+    store(0)
 
     for cp in mix_copies:
         cp.wait_recv()
@@ -329,40 +418,74 @@
     up_ag = gather(0, up_ys, up_y, up_fin)
     down_ys = exchange(1, down_rs, down_own, down_a, down_y)
 
-    for cp in back:
-        cp.wait_recv()
-    for b in range(PER):
-        rows = slice(b * BLOCK, (b + 1) * BLOCK)
-        sum_k, sum_v = parts_k[b] * factor, parts_v[b]
-        for d in range(1, REACH + 1):
-            if d == REACH and b == 0:
-                continue
-            sum_k = sum_k + got_k[d - 1, rows].astype(F32)
-            sum_v = sum_v + got_v[d - 1, rows].astype(F32)
-        dk_ref[rows] = sum_k.astype(BF)
-        dv_ref[rows] = sum_v.astype(BF)
-    out_dk = pltpu.make_async_copy(dk_ref, dk_hbm, out_sem.at[1])
-    out_dv = pltpu.make_async_copy(dv_ref, dv_hbm, out_sem.at[2])
-    out_dk.start()
-    out_dv.start()
+    came_back(1)
+
+    @pl.when(first_core)
+    def _():
+        came_back(3)
+        back[3] = (near[1] + got[1].astype(F32) + got[3].astype(F32)).astype(BF)
+        last_0.start()
+
+    @pl.when(second_core)
+    def _():
+        came_back(0, BLOCK)
+        back[3, :, :BLOCK] = (near[3, :, :BLOCK] + got[1, :, :BLOCK].astype(F32)).astype(BF)
+        back[3, :, BLOCK:] = (
+            near[3, :, BLOCK:] + got[1, :, BLOCK:].astype(F32) + got[0, :, BLOCK:].astype(F32)
+        ).astype(BF)
+        last_1.start()
 
     down_ag = gather(1, down_ys, down_y, down_fin)
+
+    @pl.when(first_core)
+    def _():
+        came_back(2)
+        near[0] = near[0] + got[2].astype(F32)
+
+    came_back(4)
+    dk_ref[...] = (near[0, 0] + got[4, 0].astype(F32)).astype(BF)
+    dv_ref[...] = (near[0, 1] + got[4, 1].astype(F32)).astype(BF)
+
     scale = (TOK * n_ctx) ** -0.5
     for cp in up_ag:
         cp.wait_recv()
     up_out[...] = up_fin[...].astype(F32) * scale
-    out_up = pltpu.make_async_copy(up_out, up_hbm, out_sem.at[3])
-    out_up.start()
     for cp in down_ag:
         cp.wait_recv()
     down_out[...] = down_fin[...].astype(F32) * scale
-    out_down = pltpu.make_async_copy(down_out, down_hbm, out_sem.at[4])
-    out_down.start()
-
-    for group in (list(halo.values()), back, mix_copies, up_rs, down_rs, up_ys, down_ys, up_ag, down_ag):
+
+    @pl.when(first_core)
+    def _():
+        for j in range(2):
+            own_far(j).wait_send()
+            pass_chip(j).wait_send()
+            pass_mate(j, 1).wait_send()
+        back_3.wait_send()
+        last_0.wait_send()
+
+    @pl.when(second_core)
+    def _():
+        for j in range(2):
+            pass_mate(j, 3).wait_send()
+        back_1.wait_send()
+        last_1.wait_send()
+
+    for j in range(2):
+        own_next(j).wait_send()
+        pass_last(j).wait_send()
+    back_4.wait_send()
+    back_2.wait_send()
+    for group in (mix_copies, up_rs, down_rs, up_ys, down_ys, up_ag, down_ag):
         for cp in group:
             cp.wait_send()
-    for cp in (out_qg, out_dk, out_dv, out_up, out_down):
+
+
+def hand_over(*refs):
+    arrays, results, sem = refs[:5], refs[5:10], refs[10]
+    out = [pltpu.make_async_copy(arrays[i], results[i], sem.at[i]) for i in range(5)]
+    for cp in out:
+        cp.start()
+    for cp in out:
         cp.wait()
 
 
@@ -379,31 +502,28 @@
     outs = pl.pallas_call(
         functools.partial(kernel, n_ctx, n_kvh),
         out_shape=(
-            jax.ShapeDtypeStruct(q.shape, BF),
-            jax.ShapeDtypeStruct(k.shape, BF),
-            jax.ShapeDtypeStruct(v.shape, BF),
-            jax.ShapeDtypeStruct((rank, feats), F32),
-            jax.ShapeDtypeStruct((rank, wide), F32),
+            pltpu.VMEM(q.shape, BF),
+            pltpu.VMEM(k.shape, BF),
+            pltpu.VMEM(v.shape, BF),
+            pltpu.VMEM((rank, feats), F32),
+            pltpu.VMEM((rank, wide), F32),
         ),
         in_specs=[anywhere] * 8,
-        out_specs=(anywhere,) * 5,
+        out_specs=(pl.BlockSpec(memory_space=pltpu.VMEM),) * 5,
         scratch_shapes=[
             vm(q.shape, BF), vm(g.shape, BF), vm(proj.shape, BF), vm((rank, TOK), BF), vm(weight.shape, BF),
             pltpu.SMEM(lengths.shape, jnp.int32),
             vm((win, HEAD), BF), vm((win, HEAD), BF), vm((HEAD, win), BF),
             vm((PER, SPAN * BLOCK, ROWS), F32), vm((PER, SPAN * BLOCK, ROWS), F32),
             vm((PER, SPAN * BLOCK, ROWS), BF), vm((PER, SPAN * BLOCK, ROWS), BF),
-            vm((PER, 8, ROWS), F32), vm(q.shape, BF),
-            vm((REACH, TOK, HEAD), BF), vm((REACH, TOK, HEAD), BF),
-            vm((REACH, TOK, HEAD), BF), vm((REACH, TOK, HEAD), BF),
-            vm(k.shape, BF), vm(v.shape, BF),
+            vm((PER, 8, ROWS), F32),
+            vm((REACH + 1, 2, TOK, HEAD), F32), vm((4, 2, TOK, HEAD), BF), vm((5, 2, TOK, HEAD), BF),
             vm((rank, TOK), F32), vm((PER, rank, BLOCK), BF), vm((PER, zs, rank, BLOCK), BF),
             vm((rank, feats), F32), vm((rank, wide), F32), vm((rank, feats), BF), vm((rank, wide), BF),
             vm((n_a, 16, feats // NCORE), BF), vm((n_a, 16, wide // NCORE), BF),
             vm((n_y, 16, feats // NCORE), BF), vm((n_y, 16, wide // NCORE), BF),
             vm((rank, feats), BF), vm((rank, wide), BF),
-            vm((rank, feats), F32), vm((rank, wide), F32),
-            dma((8,)), dma((5,)), dma((REACH, 2)), dma((REACH, 2)), dma((REACH, 2)), dma((REACH, 2)),
+            dma((8,)), dma((5, 2)), dma((REACH, 2)), dma((4,)), dma((5,)),
             dma((PER, zs)), dma((PER, zs)), dma((2, n_a)), dma((2, n_a)), dma((2, ys)), dma((2, ys)),
             dma((2, n_a)), dma((2, n_a)),
         ],
@@ -413,7 +533,15 @@
         cost_estimate=pl.CostEstimate(flops=3_200_000_000, bytes_accessed=4_000_000, transcendentals=2_400_000),
         name="attention_backward",
     )(q, k, v, g, proj, hidden.T, weight, lengths)
-    qg, dk, dv, down, up = outs
+    qg, dk, dv, down, up = pl.pallas_call(
+        hand_over,
+        out_shape=tuple(jax.ShapeDtypeStruct(o.shape, o.dtype) for o in outs),
+        in_specs=[pl.BlockSpec(memory_space=pltpu.VMEM)] * 5,
+        out_specs=(anywhere,) * 5,
+        scratch_shapes=[dma((5,))],
+        compiler_params=pltpu.CompilerParams(vmem_limit_bytes=8 * 2**20),
+        name="hand_over",
+    )(*outs)
     return qg, dk, dv, down.T, up
 
 

time: 78.6 us -> 59.6 us (0.76)
  Pallas kernels: 73 us -> 58.8 us
  local copies, waits for them, and re-layouts: 4.75 us -> 0 us
    pallas_call x1 -> x2, Pallas kernels: 73 us -> 58.8 us  [the longest x1 57.8 us: shards(): pl.pallas_call(functools.partial(kernel, n_ctx, n_kvh), out_shape=(pltpu....]
    unnamed x13 -> x0, local copies, waits for them, and re-layouts: 4.75 us -> none
where the time goes in v2:
time: 59.6 us; the launch traced here: 59.4 us
  Pallas kernels  58.8 us (99%)
  between operations  0.64 us (1%)
    pallas_call x1, Pallas kernels, shards(): pl.pallas_call(functools.partial(kernel, n_ctx, n_kvh), out_shape=(pltpu....  57.8 us

profile of v2, /device:TPU:1, one launch (start us, length us, event | category | flops | bytes accessed | tf_op | source)
XLA Modules:
  0.0 59.4 jit_solution(5363143795116389674)
XLA Ops:
  0.6 57.8 %attention_backward.1 = (bf16[384,512]{1,0:T(8,128)(2,1)S(1)}, bf16[384,128]{1,0:T(8,128)(2,1)S(1)}, bf16[384,128]{1,0:T(8,128)(2,1)S(1)}, f32[64,1024]{1,0:T(8,128)S(1)}, f32[64,512]{1,0:T(8,128)S(1)}) custom-call(bf16[384,512]{1,0:T(8,128)(2,1)} %q_hbm.1, bf16[384,128]{1,0:T(8,128)(2,1)} %k_hbm.1, bf16[384,128]{1,0:T(8,128)(2,1)} %v_hbm.1, ...), custom_call_target="tpu_custom_call" | custom-call | flops 3200000000 | bytes 4000000 | tf_op jit(solution)/shard_map/attention_backward/pallas_call | solution.py:502
  58.5 1.0 %hand_over.1 = (bf16[384,512]{1,0:T(8,128)(2,1)}, bf16[384,128]{1,0:T(8,128)(2,1)}, bf16[384,128]{1,0:T(8,128)(2,1)}, f32[64,1024]{1,0:T(8,128)}, f32[64,512]{1,0:T(8,128)}) custom-call(bf16[384,512]{1,0:T(8,128)(2,1)S(1)} %get-tuple-element.15.refs_0_, bf16[384,128]{1,0:T(8,128)(2,1)S(1)} %get-tuple-element.16.refs_1_, ...), custom_call_target="tpu_custom_call" | custom-call | tf_op jit(solution)/shard_map/hand_over/pallas_call | solution.py:536

commit v3 on v2

--- a/solution.py
+++ b/solution.py
@@ -35,11 +35,15 @@
     return op(parts, axis=0)
 
 
+def by_distance(n):
+    return sorted(range(1, n), key=lambda o: -min(o, n - o))
+
+
 def kernel(
     n_ctx, n_kvh, q_hbm, k_hbm, v_hbm, g_hbm, x_hbm, a_hbm, w_hbm, len_hbm,
     qg_ref, dk_ref, dv_ref, down_out, up_out,
     q_ref, g_ref, x_ref, a_ref, w_ref, len_ref, kwin, vwin, kwin_t, s_ref, dp_ref, p_ref, ds_ref,
-    top_ref, near, back, got,
+    top_ref, level_ref, sum_ref, near, back, got,
     mix_own, mix_send, mix_got,
     down_own, up_own, down_send, up_send, down_a, up_a, down_y, up_y, down_fin, up_fin,
     in_sem, halo_s, halo_r, back_s, back_r, mix_s, mix_r, rs_s, rs_r, ys_s, ys_r, ag_s, ag_r,
@@ -57,12 +61,11 @@
     def along(d):
         return (lax.rem(c + d + n_ctx, n_ctx), z)
 
-    z_peers = [(lax.rem(z + o, n_kvh)) for o in range(1, n_kvh)]
-    y_peers = [lax.rem(y + o, n_y) for o in range(1, n_y)]
+    z_peers = [s + (s >= z).astype(jnp.int32) for s in range(n_kvh - 1)]
+    y_peers = [lax.rem(y + o, n_y) for o in by_distance(n_y)]
     a_peers = [
-        (lax.rem(x + dx, NX), lax.rem(core + dc, NCORE))
-        for dx in range(NX) for dc in range(NCORE) if (dx, dc) != (0, 0)
-    ]
+        (lax.rem(x + dx, NX), lax.rem(core + dc, NCORE)) for dx in by_distance(NX) for dc in range(NCORE)
+    ] + [(x, 1 - core)]
 
     own = pl.ds(REACH * TOK, TOK)
     local = [
@@ -72,17 +75,17 @@
             (len_hbm, len_ref), (w_hbm, w_ref), (a_hbm, a_ref), (x_hbm, x_ref),
         ])
     ]
-    for cp in local:
-        cp.start()
     lq, lk, lg, lv, llen, lw, la, lx = local
 
     barrier = pltpu.get_barrier_semaphore()
-    greet = [along(d) for d in (1, 2, 3, -1, -2, -3)]
+    greet = [along(d) for d in (1, 3, 4, -1, -3, -4)]
     greet += [(c, zz) for zz in z_peers]
     greet += [at(yy, x, core) for yy in y_peers]
     greet += [at(y, xx, cc) for xx, cc in a_peers]
     for who in greet:
         pl.semaphore_signal(barrier, inc=1, device_id=who, device_id_type=MESH)
+    for cp in local:
+        cp.start()
     pl.semaphore_wait(barrier, len(greet))
 
     mate = along(1 - 2 * core)
@@ -100,31 +103,29 @@
     def held(j, d, first=0):
         return (kwin, vwin)[j].at[slot_rows(d, first)]
 
-    def own_next(j):
-        return forward(0, j, (k_hbm, v_hbm)[j], 1, along(1))
-
-    def own_far(j):
-        return forward(1, j, (k_hbm, v_hbm)[j], 3, along(3))
+    def own_to(j, d):
+        first = BLOCK if d == REACH else 0
+        return forward(max(d - 2, 0), j, (k_hbm, v_hbm)[j].at[pl.ds(first, TOK - first)], d, along(d), first)
 
     def pass_mate(j, d):
-        return forward(2, j, held(j, d), 2, mate)
-
-    def pass_chip(j):
-        return forward(3, j, held(j, 1), 3, along(2))
+        return forward(3, j, held(j, d), 2, mate)
 
     def pass_last(j):
-        return forward(4, j, held(j, 3, BLOCK), REACH, along(1), BLOCK)
+        return forward(4, j, held(j, 3, BLOCK), REACH, mate, BLOCK)
 
     def arrived(j, d):
         first = BLOCK if d == REACH else 0
         forward(0, j, held(j, d, first), d, along(1), first).wait_recv()
 
-    for j in range(2):
-        own_next(j).start()
-
-        @pl.when(first_core)
-        def _(j=j):
-            own_far(j).start()
+    @pl.when(first_core)
+    def _():
+        for d, j in ((3, 0), (1, 0), (3, 1), (1, 1), (4, 0), (4, 1)):
+            own_to(j, d).start()
+
+    @pl.when(second_core)
+    def _():
+        for d, j in ((1, 0), (1, 1), (3, 0), (3, 1)):
+            own_to(j, d).start()
 
     llen.wait()
     firsts = [jnp.int32(0)] * PER
@@ -183,82 +184,113 @@
                 vwin[lo * BLOCK:hi * BLOCK], rows_of(g_ref, i), NT
             )
 
+    factor = HEAD ** -0.5
+    rate = factor * math.log2(math.e)
+    STEP = 64
+    zero = jnp.zeros((8, ROWS), F32)
+
+    def weights(d):
+        for i in range(PER):
+            lo, hi = window(d, i)
+            if lo >= hi:
+                continue
+            top = jnp.max(top_ref[i], axis=0, keepdims=True)
+            level_ref[d, i] = jnp.broadcast_to(top, (8, ROWS))
+            total, delta = zero, zero
+            for w in range(lo, hi):
+                slot = w - i - 1
+                level = top + away(i, slot)
+
+                def weigh(t, carry, i=i, slot=slot, level=level):
+                    total, delta = carry
+                    span = pl.ds(pl.multiple_of(slot * BLOCK + t * STEP, STEP), STEP)
+                    p = jnp.exp2((s_ref[i, span] - level) * rate)
+                    s_ref[i, span] = p
+                    return total + fold8(p, jnp.sum), delta + fold8(p * dp_ref[i, span], jnp.sum)
+
+                total, delta = lax.fori_loop(0, BLOCK // STEP, weigh, (total, delta), unroll=True)
+            sum_ref[d, i, 0] = total
+            sum_ref[d, i, 1] = delta
+
+    def attend(d):
+        scores(d)
+        dprobs(d)
+        weights(d)
+
     lq.wait()
     lk.wait()
-    scores(0)
     lg.wait()
     lv.wait()
-    dprobs(0)
+    attend(0)
 
     @pl.when(second_core)
     def _():
         for j in range(2):
             arrived(j, 1)
-        scores(1)
-        dprobs(1)
+        attend(1)
+        for j in range(2):
+            arrived(j, 3)
+            pass_mate(j, 3).start()
+        attend(3)
+
+    @pl.when(first_core)
+    def _():
+        for j in range(2):
+            arrived(j, 1)
+            pass_mate(j, 1).start()
+        attend(1)
+
+    for j in range(2):
+        arrived(j, 2)
+    attend(2)
+
+    @pl.when(first_core)
+    def _():
         for j in range(2):
             arrived(j, 3)
             pass_last(j).start()
-            pass_mate(j, 3).start()
-        scores(3)
-        dprobs(3)
-
-    @pl.when(first_core)
-    def _():
-        for j in range(2):
-            arrived(j, 1)
-            pass_chip(j).start()
-            pass_mate(j, 1).start()
-        scores(1)
-        dprobs(1)
-
-    for j in range(2):
-        arrived(j, 2)
-    scores(2)
-    dprobs(2)
-
-    @pl.when(first_core)
-    def _():
-        for j in range(2):
-            arrived(j, 3)
-            pass_last(j).start()
-        scores(3)
-        dprobs(3)
-
-    arrived(0, REACH)
-    scores(REACH)
-    arrived(1, REACH)
-    dprobs(REACH)
-
-    factor = HEAD ** -0.5
-    rate = factor * math.log2(math.e)
-    STEP = 64
-    lw.wait()
+        attend(3)
+
     mix_copies = []
-    for i in range(PER):
+
+    def mix_copy(i, s):
+        slot = z - (z > z_peers[s]).astype(jnp.int32)
+        return pltpu.make_async_remote_copy(
+            src_ref=mix_send.at[i], dst_ref=mix_got.at[i, slot],
+            send_sem=mix_s.at[i, s], recv_sem=mix_r.at[i, slot],
+            device_id=(c, z_peers[s]), device_id_type=MESH,
+        )
+
+    def mix_arrived(i, s):
+        pltpu.make_async_remote_copy(
+            src_ref=mix_send.at[i], dst_ref=mix_got.at[i, s],
+            send_sem=mix_s.at[i, s], recv_sem=mix_r.at[i, s],
+            device_id=(c, z_peers[s]), device_id_type=MESH,
+        ).wait_recv()
+
+    def finish(i):
         top = jnp.max(top_ref[i], axis=0, keepdims=True)
-
-        def weigh(t, carry, i=i, top=top):
-            total, delta = carry
-            span = pl.ds(pl.multiple_of(t * STEP, STEP), STEP)
-            level = top + away(i, t * STEP // BLOCK)
-            p = jnp.exp2((s_ref[i, span] - level) * rate)
-            s_ref[i, span] = p
-            return total + fold8(p, jnp.sum), delta + fold8(p * dp_ref[i, span], jnp.sum)
-
-        zero = jnp.zeros((8, ROWS), F32)
-        total, delta = lax.fori_loop(0, SPAN * BLOCK // STEP, weigh, (zero, zero))
+        near_ranges = [d for d in range(REACH + 1) if window(d, i)[0] < window(d, i)[1]]
+        fades = {d: jnp.exp2((level_ref[d, i, :1] - top) * rate) for d in near_ranges}
+        total, delta = zero, zero
+        for d in near_ranges:
+            total = total + sum_ref[d, i, 0] * fades[d]
+            delta = delta + sum_ref[d, i, 1] * fades[d]
         share = 1.0 / jnp.sum(total, axis=0, keepdims=True)
         delta = jnp.sum(delta, axis=0, keepdims=True) * share
-
-        def settle(t, carry, i=i, share=share, delta=delta):
-            span = pl.ds(pl.multiple_of(t * STEP, STEP), STEP)
-            p = s_ref[i, span] * share
-            p_ref[i, span] = p.astype(BF)
-            ds_ref[i, span] = (p * (dp_ref[i, span] - delta)).astype(BF)
-            return carry
-
-        lax.fori_loop(0, SPAN * BLOCK // STEP, settle, 0)
+        for d in near_ranges:
+            lo, hi = window(d, i)
+            start = (lo - i - 1) * BLOCK
+            part = fades[d] * share
+            level_ref[d, i] = jnp.broadcast_to(part, (8, ROWS))
+
+            def settle(t, carry, i=i, start=start, part=part, delta=delta):
+                span = pl.ds(pl.multiple_of(start + t * STEP, STEP), STEP)
+                p = s_ref[i, span] * part
+                ds_ref[i, span] = (p * (dp_ref[i, span] - delta)).astype(BF)
+                return carry
+
+            lax.fori_loop(0, (hi - lo) * BLOCK // STEP, settle, 0)
         dq = dot(kwin_t[:, (i + 1) * BLOCK:(i + 1 + SPAN) * BLOCK], ds_ref[i]) * factor
         for h in range(HEADS):
             qg_ref[i * BLOCK:(i + 1) * BLOCK, h * HEAD:(h + 1) * HEAD] = (
@@ -267,14 +299,18 @@
         mixed = dot(w_ref[...], qg_ref[i * BLOCK:(i + 1) * BLOCK], NT)
         mix_own[:, i * BLOCK:(i + 1) * BLOCK] = mixed
         mix_send[i] = mixed.astype(BF)
-        for o, zz in enumerate(z_peers):
-            cp = pltpu.make_async_remote_copy(
-                src_ref=mix_send.at[i], dst_ref=mix_got.at[i, o],
-                send_sem=mix_s.at[i, o], recv_sem=mix_r.at[i, o],
-                device_id=(c, zz), device_id_type=MESH,
-            )
+        for n in range(n_kvh - 1):
+            cp = mix_copy(i, n)
             cp.start()
             mix_copies.append(cp)
+
+    lw.wait()
+    finish(2)
+    for j in range(2):
+        arrived(j, REACH)
+    attend(REACH)
+    finish(1)
+    finish(0)
 
     def chunk(ref, xx, cc):
         width = ref.shape[1] // NCORE
@@ -336,6 +372,19 @@
     up_rs = scatter(0, up_send, up_a)
 
     def ranges(d):
+        for i in range(PER):
+            lo, hi = window(d, i)
+            if lo >= hi:
+                continue
+            start = (lo - i - 1) * BLOCK
+            part = level_ref[d, i, :1]
+
+            def normal(t, carry, i=i, start=start, part=part):
+                span = pl.ds(pl.multiple_of(start + t * STEP, STEP), STEP)
+                p_ref[i, span] = (s_ref[i, span] * part).astype(BF)
+                return carry
+
+            lax.fori_loop(0, (hi - lo) * BLOCK // STEP, normal, 0)
         low = (REACH - d) * PER
         dk = jnp.zeros((TOK, HEAD), F32)
         dv = jnp.zeros((TOK, HEAD), F32)
@@ -400,23 +449,25 @@
         back[2, :, BLOCK:] = (near[3, :, BLOCK:] + got[0, :, BLOCK:].astype(F32)).astype(BF)
         back_3.start()
 
+    store(0)
+
+    lx.wait()
+    for i in range(PER - 1, -1, -1):
+        cols = slice(i * BLOCK, (i + 1) * BLOCK)
+        mixed = mix_own[:, cols]
+        for n in range(n_kvh - 1):
+            mix_arrived(i, n)
+            mixed = mixed + mix_got[i, n].astype(F32)
+        part = dot(mixed.astype(BF), x_ref[cols])
+        if i < PER - 1:
+            part = part + down_own[...]
+        down_own[...] = part
+        if i == 0:
+            down_send[...] = part.astype(BF)
+    down_rs = scatter(1, down_send, down_a)
     up_ys = exchange(0, up_rs, up_own, up_a, up_y)
-
-    store(0)
-
-    for cp in mix_copies:
-        cp.wait_recv()
-    lx.wait()
-    mixed = mix_own[...]
-    for o in range(n_kvh - 1):
-        mixed = mixed + jnp.concatenate([mix_got[i, o].astype(F32) for i in range(PER)], axis=1)
-    down = dot(mixed.astype(BF), x_ref[...])
-    down_own[...] = down
-    down_send[...] = down.astype(BF)
-    down_rs = scatter(1, down_send, down_a)
-
+    down_ys = exchange(1, down_rs, down_own, down_a, down_y)
     up_ag = gather(0, up_ys, up_y, up_fin)
-    down_ys = exchange(1, down_rs, down_own, down_a, down_y)
 
     came_back(1)
 
@@ -457,9 +508,9 @@
     @pl.when(first_core)
     def _():
         for j in range(2):
-            own_far(j).wait_send()
-            pass_chip(j).wait_send()
+            own_to(j, REACH).wait_send()
             pass_mate(j, 1).wait_send()
+            pass_last(j).wait_send()
         back_3.wait_send()
         last_0.wait_send()
 
@@ -471,8 +522,8 @@
         last_1.wait_send()
 
     for j in range(2):
-        own_next(j).wait_send()
-        pass_last(j).wait_send()
+        own_to(j, 1).wait_send()
+        own_to(j, 3).wait_send()
     back_4.wait_send()
     back_2.wait_send()
     for group in (mix_copies, up_rs, down_rs, up_ys, down_ys, up_ag, down_ag):
@@ -516,7 +567,7 @@
             vm((win, HEAD), BF), vm((win, HEAD), BF), vm((HEAD, win), BF),
             vm((PER, SPAN * BLOCK, ROWS), F32), vm((PER, SPAN * BLOCK, ROWS), F32),
             vm((PER, SPAN * BLOCK, ROWS), BF), vm((PER, SPAN * BLOCK, ROWS), BF),
-            vm((PER, 8, ROWS), F32),
+            vm((PER, 8, ROWS), F32), vm((REACH + 1, PER, 8, ROWS), F32), vm((REACH + 1, PER, 2, 8, ROWS), F32),
             vm((REACH + 1, 2, TOK, HEAD), F32), vm((4, 2, TOK, HEAD), BF), vm((5, 2, TOK, HEAD), BF),
             vm((rank, TOK), F32), vm((PER, rank, BLOCK), BF), vm((PER, zs, rank, BLOCK), BF),
             vm((rank, feats), F32), vm((rank, wide), F32), vm((rank, feats), BF), vm((rank, wide), BF),

time: 59.6 us -> 57 us (0.956)
  Pallas kernels: 58.8 us -> 56.2 us
    pallas_call x1, Pallas kernels: 57.8 us -> 55.2 us  [shards(): pl.pallas_call(functools.partial(kernel, n_ctx, n_kvh), out_shape=(pltpu....]
where the time goes in v3:
time: 57 us; the launch traced here: 56.8 us
  Pallas kernels  56.2 us (99%)
  between operations  0.64 us (1%)
    pallas_call x1, Pallas kernels, shards(): pl.pallas_call(functools.partial(kernel, n_ctx, n_kvh), out_shape=(pltpu....  55.2 us

profile of v3, /device:TPU:1, one launch (start us, length us, event | category | flops | bytes accessed | tf_op | source)
XLA Modules:
  0.0 56.8 jit_solution(17608377593548181710)
XLA Ops:
  0.6 55.2 %attention_backward.1 = (bf16[384,512]{1,0:T(8,128)(2,1)S(1)}, bf16[384,128]{1,0:T(8,128)(2,1)S(1)}, bf16[384,128]{1,0:T(8,128)(2,1)S(1)}, f32[64,1024]{1,0:T(8,128)S(1)}, f32[64,512]{1,0:T(8,128)S(1)}) custom-call(bf16[384,512]{1,0:T(8,128)(2,1)} %q_hbm.1, bf16[384,128]{1,0:T(8,128)(2,1)} %k_hbm.1, bf16[384,128]{1,0:T(8,128)(2,1)} %v_hbm.1, ...), custom_call_target="tpu_custom_call" | custom-call | flops 3200000000 | bytes 4000000 | tf_op jit(solution)/shard_map/attention_backward/pallas_call | solution.py:553
  55.9 1.0 %hand_over.1 = (bf16[384,512]{1,0:T(8,128)(2,1)}, bf16[384,128]{1,0:T(8,128)(2,1)}, bf16[384,128]{1,0:T(8,128)(2,1)}, f32[64,1024]{1,0:T(8,128)}, f32[64,512]{1,0:T(8,128)}) custom-call(bf16[384,512]{1,0:T(8,128)(2,1)S(1)} %get-tuple-element.15.refs_0_, bf16[384,128]{1,0:T(8,128)(2,1)S(1)} %get-tuple-element.16.refs_1_, ...), custom_call_target="tpu_custom_call" | custom-call | tf_op jit(solution)/shard_map/hand_over/pallas_call | solution.py:587

commit v4 on v3

--- a/solution.py
+++ b/solution.py
@@ -42,7 +42,7 @@
 def kernel(
     n_ctx, n_kvh, q_hbm, k_hbm, v_hbm, g_hbm, x_hbm, a_hbm, w_hbm, len_hbm,
     qg_ref, dk_ref, dv_ref, down_out, up_out,
-    q_ref, g_ref, x_ref, a_ref, w_ref, len_ref, kwin, vwin, kwin_t, s_ref, dp_ref, p_ref, ds_ref,
+    q_ref, g_ref, x_ref, a_ref, w_ref, len_ref, kwin, vwin, relay, kwin_t, s_ref, dp_ref, p_ref, ds_ref,
     top_ref, level_ref, sum_ref, near, back, got,
     mix_own, mix_send, mix_got,
     down_own, up_own, down_send, up_send, down_a, up_a, down_y, up_y, down_fin, up_fin,
@@ -78,7 +78,7 @@
     lq, lk, lg, lv, llen, lw, la, lx = local
 
     barrier = pltpu.get_barrier_semaphore()
-    greet = [along(d) for d in (1, 3, 4, -1, -3, -4)]
+    greet = [along(d) for d in (1, 3, 6, -1, -3, -6)]
     greet += [(c, zz) for zz in z_peers]
     greet += [at(yy, x, core) for yy in y_peers]
     greet += [at(y, xx, cc) for xx, cc in a_peers]
@@ -104,8 +104,18 @@
         return (kwin, vwin)[j].at[slot_rows(d, first)]
 
     def own_to(j, d):
-        first = BLOCK if d == REACH else 0
-        return forward(max(d - 2, 0), j, (k_hbm, v_hbm)[j].at[pl.ds(first, TOK - first)], d, along(d), first)
+        return forward(d // 2, j, (k_hbm, v_hbm)[j], d, along(d))
+
+    def own_round(j):
+        return pltpu.make_async_remote_copy(
+            src_ref=(k_hbm, v_hbm)[j].at[pl.ds(BLOCK, TOK - BLOCK)], dst_ref=relay.at[j],
+            send_sem=halo_s.at[2, j], recv_sem=halo_r.at[REACH, j],
+            device_id=at(y, lax.rem(x + NX - 1, NX), core), device_id_type=MESH,
+        )
+
+    def pass_round(j):
+        to = along(jnp.where(x == NX - 1, -2, 6))
+        return forward(5, j, relay.at[j], REACH, to, BLOCK)
 
     def pass_mate(j, d):
         return forward(3, j, held(j, d), 2, mate)
@@ -119,8 +129,10 @@
 
     @pl.when(first_core)
     def _():
-        for d, j in ((3, 0), (1, 0), (3, 1), (1, 1), (4, 0), (4, 1)):
+        for d, j in ((3, 0), (1, 0), (3, 1), (1, 1)):
             own_to(j, d).start()
+            if d == 3:
+                own_round(j).start()
 
     @pl.when(second_core)
     def _():
@@ -238,6 +250,9 @@
         for j in range(2):
             arrived(j, 1)
             pass_mate(j, 1).start()
+        for j in range(2):
+            own_round(j).wait_recv()
+            pass_round(j).start()
         attend(1)
 
     for j in range(2):
@@ -431,25 +446,27 @@
     store(REACH)
     back[0, :, BLOCK:] = near[REACH, :, BLOCK:].astype(BF)
     back_4.start()
+    store(3)
+
+    @pl.when(first_core)
+    def _():
+        came_back(0, BLOCK)
+        back[2, :, :BLOCK] = near[3, :, :BLOCK].astype(BF)
+        back[2, :, BLOCK:] = (near[3, :, BLOCK:] + got[0, :, BLOCK:].astype(F32)).astype(BF)
+        back_3.start()
+
     store(2)
     back[1] = near[2].astype(BF)
     back_2.start()
     store(1)
-    store(3)
 
     @pl.when(second_core)
     def _():
         back[2] = near[1].astype(BF)
         back_1.start()
 
-    @pl.when(first_core)
-    def _():
-        came_back(0, BLOCK)
-        back[2, :, :BLOCK] = near[3, :, :BLOCK].astype(BF)
-        back[2, :, BLOCK:] = (near[3, :, BLOCK:] + got[0, :, BLOCK:].astype(F32)).astype(BF)
-        back_3.start()
-
     store(0)
+    up_ys = exchange(0, up_rs, up_own, up_a, up_y)
 
     lx.wait()
     for i in range(PER - 1, -1, -1):
@@ -465,9 +482,7 @@
         if i == 0:
             down_send[...] = part.astype(BF)
     down_rs = scatter(1, down_send, down_a)
-    up_ys = exchange(0, up_rs, up_own, up_a, up_y)
     down_ys = exchange(1, down_rs, down_own, down_a, down_y)
-    up_ag = gather(0, up_ys, up_y, up_fin)
 
     came_back(1)
 
@@ -486,6 +501,7 @@
         ).astype(BF)
         last_1.start()
 
+    up_ag = gather(0, up_ys, up_y, up_fin)
     down_ag = gather(1, down_ys, down_y, down_fin)
 
     @pl.when(first_core)
@@ -508,7 +524,8 @@
     @pl.when(first_core)
     def _():
         for j in range(2):
-            own_to(j, REACH).wait_send()
+            own_round(j).wait_send()
+            pass_round(j).wait_send()
             pass_mate(j, 1).wait_send()
             pass_last(j).wait_send()
         back_3.wait_send()
@@ -564,7 +581,7 @@
         scratch_shapes=[
             vm(q.shape, BF), vm(g.shape, BF), vm(proj.shape, BF), vm((rank, TOK), BF), vm(weight.shape, BF),
             pltpu.SMEM(lengths.shape, jnp.int32),
-            vm((win, HEAD), BF), vm((win, HEAD), BF), vm((HEAD, win), BF),
+            vm((win, HEAD), BF), vm((win, HEAD), BF), vm((2, TOK - BLOCK, HEAD), BF), vm((HEAD, win), BF),
             vm((PER, SPAN * BLOCK, ROWS), F32), vm((PER, SPAN * BLOCK, ROWS), F32),
             vm((PER, SPAN * BLOCK, ROWS), BF), vm((PER, SPAN * BLOCK, ROWS), BF),
             vm((PER, 8, ROWS), F32), vm((REACH + 1, PER, 8, ROWS), F32), vm((REACH + 1, PER, 2, 8, ROWS), F32),
@@ -574,7 +591,7 @@
             vm((n_a, 16, feats // NCORE), BF), vm((n_a, 16, wide // NCORE), BF),
             vm((n_y, 16, feats // NCORE), BF), vm((n_y, 16, wide // NCORE), BF),
             vm((rank, feats), BF), vm((rank, wide), BF),
-            dma((8,)), dma((5, 2)), dma((REACH, 2)), dma((4,)), dma((5,)),
+            dma((8,)), dma((6, 2)), dma((REACH + 1, 2)), dma((4,)), dma((5,)),
             dma((PER, zs)), dma((PER, zs)), dma((2, n_a)), dma((2, n_a)), dma((2, ys)), dma((2, ys)),
             dma((2, n_a)), dma((2, n_a)),
         ],

time: 57 us -> 55.7 us (0.977)
  Pallas kernels: 56.2 us -> 55 us
    pallas_call x1, Pallas kernels: 55.2 us -> 54 us  [shards(): pl.pallas_call(functools.partial(kernel, n_ctx, n_kvh), out_shape=(pltpu....]
where the time goes in v4:
time: 55.7 us; the launch traced here: 55.6 us
  Pallas kernels  55 us (99%)
  between operations  0.64 us (1%)
    pallas_call x1, Pallas kernels, shards(): pl.pallas_call(functools.partial(kernel, n_ctx, n_kvh), out_shape=(pltpu....  54 us

profile of v4, /device:TPU:1, one launch (start us, length us, event | category | flops | bytes accessed | tf_op | source)
XLA Modules:
  0.0 55.6 jit_solution(17945515565991755308)
XLA Ops:
  0.6 54.0 %attention_backward.1 = (bf16[384,512]{1,0:T(8,128)(2,1)S(1)}, bf16[384,128]{1,0:T(8,128)(2,1)S(1)}, bf16[384,128]{1,0:T(8,128)(2,1)S(1)}, f32[64,1024]{1,0:T(8,128)S(1)}, f32[64,512]{1,0:T(8,128)S(1)}) custom-call(bf16[384,512]{1,0:T(8,128)(2,1)} %q_hbm.1, bf16[384,128]{1,0:T(8,128)(2,1)} %k_hbm.1, bf16[384,128]{1,0:T(8,128)(2,1)} %v_hbm.1, ...), custom_call_target="tpu_custom_call" | custom-call | flops 3200000000 | bytes 4000000 | tf_op jit(solution)/shard_map/attention_backward/pallas_call | solution.py:570
  54.6 1.0 %hand_over.1 = (bf16[384,512]{1,0:T(8,128)(2,1)}, bf16[384,128]{1,0:T(8,128)(2,1)}, bf16[384,128]{1,0:T(8,128)(2,1)}, f32[64,1024]{1,0:T(8,128)}, f32[64,512]{1,0:T(8,128)}) custom-call(bf16[384,512]{1,0:T(8,128)(2,1)S(1)} %get-tuple-element.15.refs_0_, bf16[384,128]{1,0:T(8,128)(2,1)S(1)} %get-tuple-element.16.refs_1_, ...), custom_call_target="tpu_custom_call" | custom-call | tf_op jit(solution)/shard_map/hand_over/pallas_call | solution.py:604

commit v5 on v4

--- a/solution.py
+++ b/solution.py
@@ -62,7 +62,7 @@
         return (lax.rem(c + d + n_ctx, n_ctx), z)
 
     z_peers = [s + (s >= z).astype(jnp.int32) for s in range(n_kvh - 1)]
-    y_peers = [lax.rem(y + o, n_y) for o in by_distance(n_y)]
+    y_peers = [s + (s >= y).astype(jnp.int32) for s in range(n_y - 1)]
     a_peers = [
         (lax.rem(x + dx, NX), lax.rem(core + dc, NCORE)) for dx in by_distance(NX) for dc in range(NCORE)
     ] + [(x, 1 - core)]
@@ -305,7 +305,7 @@
                 ds_ref[i, span] = (p * (dp_ref[i, span] - delta)).astype(BF)
                 return carry
 
-            lax.fori_loop(0, (hi - lo) * BLOCK // STEP, settle, 0)
+            lax.fori_loop(0, (hi - lo) * BLOCK // STEP, settle, 0, unroll=True)
         dq = dot(kwin_t[:, (i + 1) * BLOCK:(i + 1 + SPAN) * BLOCK], ds_ref[i]) * factor
         for h in range(HEADS):
             qg_ref[i * BLOCK:(i + 1) * BLOCK, h * HEAD:(h + 1) * HEAD] = (
@@ -343,6 +343,13 @@
             copies.append(cp)
         return copies
 
+    def y_copy(which, o, mark, slots):
+        return pltpu.make_async_remote_copy(
+            src_ref=slots.at[y], dst_ref=slots.at[y],
+            send_sem=ys_s.at[which, o], recv_sem=ys_r.at[which, mark],
+            device_id=at(y_peers[o], x, core), device_id_type=MESH,
+        )
+
     def exchange(which, copies, own_part, got, slots):
         for cp in copies:
             cp.wait_recv()
@@ -351,19 +358,15 @@
             part = part + got[o].astype(F32)
         slots[y] = part.astype(BF)
         out = []
-        for o, yy in enumerate(y_peers):
-            cp = pltpu.make_async_remote_copy(
-                src_ref=slots.at[y], dst_ref=slots.at[y],
-                send_sem=ys_s.at[which, o], recv_sem=ys_r.at[which, o],
-                device_id=at(yy, x, core), device_id_type=MESH,
-            )
+        for o in range(n_y - 1):
+            cp = y_copy(which, o, y - (y > y_peers[o]).astype(jnp.int32), slots)
             cp.start()
             out.append(cp)
         return out
 
-    def gather(which, copies, slots, fin):
-        for cp in copies:
-            cp.wait_recv()
+    def gather(which, slots, fin):
+        for o in range(n_y - 1):
+            y_copy(which, o, o, slots).wait_recv()
         part = slots[0].astype(F32)
         for yy in range(1, n_y):
             part = part + slots[yy].astype(F32)
@@ -501,8 +504,8 @@
         ).astype(BF)
         last_1.start()
 
-    up_ag = gather(0, up_ys, up_y, up_fin)
-    down_ag = gather(1, down_ys, down_y, down_fin)
+    up_ag = gather(0, up_y, up_fin)
+    down_ag = gather(1, down_y, down_fin)
 
     @pl.when(first_core)
     def _():

time: 55.7 us -> 55.4 us (level)
  no operation moved by 1% of the time
where the time goes in v5:
time: 55.4 us; the launch traced here: 55.2 us
  Pallas kernels  54.5 us (98%)
  between operations  0.64 us (1%)
    pallas_call x1, Pallas kernels, shards(): pl.pallas_call(functools.partial(kernel, n_ctx, n_kvh), out_shape=(pltpu....  53.5 us

profile of v5, /device:TPU:1, one launch (start us, length us, event | category | flops | bytes accessed | tf_op | source)
XLA Modules:
  0.0 55.2 jit_solution(4847518158291030769)
XLA Ops:
  0.6 53.5 %attention_backward.1 = (bf16[384,512]{1,0:T(8,128)(2,1)S(1)}, bf16[384,128]{1,0:T(8,128)(2,1)S(1)}, bf16[384,128]{1,0:T(8,128)(2,1)S(1)}, f32[64,1024]{1,0:T(8,128)S(1)}, f32[64,512]{1,0:T(8,128)S(1)}) custom-call(bf16[384,512]{1,0:T(8,128)(2,1)} %q_hbm.1, bf16[384,128]{1,0:T(8,128)(2,1)} %k_hbm.1, bf16[384,128]{1,0:T(8,128)(2,1)} %v_hbm.1, ...), custom_call_target="tpu_custom_call" | custom-call | flops 3200000000 | bytes 4000000 | tf_op jit(solution)/shard_map/attention_backward/pallas_call | solution.py:573
  54.2 1.0 %hand_over.1 = (bf16[384,512]{1,0:T(8,128)(2,1)}, bf16[384,128]{1,0:T(8,128)(2,1)}, bf16[384,128]{1,0:T(8,128)(2,1)}, f32[64,1024]{1,0:T(8,128)}, f32[64,512]{1,0:T(8,128)}) custom-call(bf16[384,512]{1,0:T(8,128)(2,1)S(1)} %get-tuple-element.15.refs_0_, bf16[384,128]{1,0:T(8,128)(2,1)S(1)} %get-tuple-element.16.refs_1_, ...), custom_call_target="tpu_custom_call" | custom-call | tf_op jit(solution)/shard_map/hand_over/pallas_call | solution.py:607
